TPU v7x, 32 devices: a whole 2x2x4 slice. The times are simulated.
32 devices in a mesh: seq: 8 (over y, x, core), tp: 4 (over z).
Axes of the slice: x: 2, y: 2, z: 4, core: 2. Of those that a mesh axis runs over, the one named last changes fastest.
Arguments:
- queries: bfloat16 [4096, 6144], P('seq', 'tp'), may hold values from -6 to 6
- keys: bfloat16 [4096, 1024], P('seq', 'tp'), may hold values from -6 to 6
- values: bfloat16 [4096, 1024], P('seq', 'tp'), may hold values from -6 to 6
- segment_ids: int32 [4096], replicated, may hold values from 0 to 3, never falling along the last dimension, each value on 1 to 3072 neighbouring positions
- packing: int32 [32, 2], replicated, may hold values from 0 to 7, as said below
- out_weight: bfloat16 [6144, 12288], P('tp', 'seq'), may hold values from -0.625 to 0.625
Outputs:
- attended: bfloat16 [4096, 12288], P('seq', 'tp')
Inputs may be any that keep to these rules, and one draw needn't show every extreme that they name: `packing`: each arriving block gets a distinct packed place, so every packed shard receives exactly 4 blocks at offsets 0 to 3; the blocks of one shard go to 4 different packed shards. `segment_ids`: document ids never fall along the tokens; each document has 1 to 3072 tokens and one has exactly 3072.
All inputs are finite; a program needn't handle non-finite values.
Results may differ from a plain program's by a relative error of at most 0.015.
Values may be sent and summed in bfloat16 or wider, within the bound.
No kernel may reach another device: no remote copies, remote signals or barrier semaphores. Data moves between devices by JAX's collectives and lax.ppermute only.
A program may use at most 128 MiB of HBM per device.

v0:
```python
import math

import jax
import jax.numpy as jnp
from jax import lax
from jax.sharding import PartitionSpec as P

HEAD_DIM = 128
WINDOW = 4096
BLOCK = 128


def passed_along(block, axis, distance):
    devices = range(lax.axis_size(axis))
    route = [(i - distance, i) for i in devices if i - distance in devices]
    return lax.ppermute(block, axis, route)


def attend_head(q_rows, k_rows, v_rows, q_pos, k_pos, q_seg, k_seg):
    scores = lax.dot_general(
        q_rows, k_rows, (((1,), (1,)), ((), ())), preferred_element_type=jnp.float32
    )
    scores = scores * (1.0 / math.sqrt(HEAD_DIM))
    allowed = (k_pos[None, :] <= q_pos[:, None]) & (k_pos[None, :] > q_pos[:, None] - WINDOW)
    allowed = allowed & (k_seg[None, :] == q_seg[:, None])
    scores = jnp.where(allowed, scores, -jnp.inf)
    top_score = jnp.max(scores, axis=1, keepdims=True)
    expo = jnp.exp(scores - top_score)
    weights = (expo / jnp.sum(expo, axis=1, keepdims=True)).astype(jnp.bfloat16)
    return jnp.dot(weights, v_rows, preferred_element_type=jnp.float32).astype(jnp.bfloat16)


def shards(queries, keys, values, segment_ids, packing, out_weight):
    tok_rows = queries.shape[0]
    q_cols = queries.shape[1]
    kv_cols = keys.shape[1]
    seq_count = lax.axis_size("seq")
    shard_index = lax.axis_index("seq")
    per_shard = tok_rows // BLOCK
    blocks_all = packing.shape[0]
    joined = jnp.concatenate([queries, keys, values], axis=1)
    row_width = joined.shape[1]
    own_blocks = joined.reshape(per_shard, BLOCK, row_width)
    own_list = lax.dynamic_slice_in_dim(packing, shard_index * per_shard, per_shard, 0)
    slot_ids = jnp.arange(seq_count, dtype=jnp.int32)
    routing = (own_list[:, 0][None, :] == slot_ids[:, None]).astype(jnp.bfloat16)
    outgoing = jnp.einsum(
        "db,brc->drc", routing, own_blocks, preferred_element_type=jnp.float32
    ).astype(jnp.bfloat16)
    incoming = lax.all_to_all(outgoing, "seq", split_axis=0, concat_axis=0, tiled=True)
    arriving = packing[:, 0] == shard_index
    offset_ids = jnp.arange(per_shard, dtype=jnp.int32)
    at_offset = ((packing[:, 1][None, :] == offset_ids[:, None]) & arriving[None, :]).astype(
        jnp.float32
    )
    senders = jnp.arange(blocks_all, dtype=jnp.int32) // per_shard
    from_sender = (senders[:, None] == slot_ids[None, :]).astype(jnp.float32)
    placing = jnp.dot(at_offset, from_sender, precision=lax.Precision.HIGHEST).astype(jnp.bfloat16)
    packed = jnp.einsum(
        "od,drc->orc", placing, incoming, preferred_element_type=jnp.float32
    ).astype(jnp.bfloat16)
    packed = packed.reshape(tok_rows, row_width)
    queries_here = packed[:, :q_cols]
    key_values = packed[:, q_cols:]
    span_shards = WINDOW // tok_rows
    earlier_pieces = []
    for distance in range(span_shards, 0, -1):
        earlier_pieces.append(passed_along(key_values, "seq", distance))
    context = jnp.concatenate(earlier_pieces + [key_values], axis=0)
    ctx_keys = context[:, :kv_cols]
    ctx_values = context[:, kv_cols:]
    ctx_rows = context.shape[0]
    q_pos = shard_index * tok_rows + jnp.arange(tok_rows, dtype=jnp.int32)
    k_pos = (shard_index - span_shards) * tok_rows + jnp.arange(ctx_rows, dtype=jnp.int32)
    padded_seg = jnp.concatenate([jnp.full((WINDOW,), -1, jnp.int32), segment_ids], axis=0)
    q_seg = lax.dynamic_slice_in_dim(segment_ids, shard_index * tok_rows, tok_rows, 0)
    k_seg = lax.dynamic_slice_in_dim(padded_seg, shard_index * tok_rows, ctx_rows, 0)
    heads_here = q_cols // HEAD_DIM
    group_size = heads_here // (kv_cols // HEAD_DIM)

    def one_head(head_index):
        q_head = lax.dynamic_slice_in_dim(queries_here, head_index * HEAD_DIM, HEAD_DIM, 1)
        kv_start = head_index // group_size * HEAD_DIM
        k_head = lax.dynamic_slice_in_dim(ctx_keys, kv_start, HEAD_DIM, 1)
        v_head = lax.dynamic_slice_in_dim(ctx_values, kv_start, HEAD_DIM, 1)
        return attend_head(q_head, k_head, v_head, q_pos, k_pos, q_seg, k_seg)

    per_head = lax.map(one_head, jnp.arange(heads_here, dtype=jnp.int32))
    attended = jnp.transpose(per_head, (1, 0, 2)).reshape(tok_rows, q_cols)
    terms = jnp.dot(
        attended,
        lax.all_gather(out_weight, "seq", axis=1, tiled=True),
        preferred_element_type=jnp.float32,
    )
    result = lax.psum_scatter(terms.astype(jnp.bfloat16), "tp", scatter_dimension=1, tiled=True)
    return result


def solution(mesh):
    in_specs = (P("seq", "tp"), P("seq", "tp"), P("seq", "tp"), P(), P(), P("tp", "seq"))
    out_specs = P("seq", "tp")
    return jax.shard_map(shards, mesh=mesh, in_specs=in_specs, out_specs=out_specs, check_vma=False)
```

profile of v0, /device:TPU:0, one launch (start us, length us, event | category | flops | bytes accessed | tf_op | source)
XLA Modules:
  0.0 593.2 jit_solution(11790392605664629646)
XLA Ops:
  8.3 2.3 convolution_convert_fusion.1
  10.7 4.2 copy.14
  14.9 5.2 all-to-all-start
  20.3 90.0 %all-to-all-done = bf16[8,128,2048]{2,1,0:T(8,128)(2,1)} async-done(((bf16[8,128,2048]{2,1,0:T(8,128)(2,1)}), bf16[8,128,2048]{2,1,0:T(8,128)(2,1)}, u32[]{:S(2)}, u32[]{:S(2)}) %all-to-all-start) | async-done | bytes 4194336 | tf_op jit(solution)/shard_map/all_to_all | solution.py:50
  110.3 5.3 fusion.19
  118.2 2.1 collective-permute-start.1
  120.4 2.7 collective-permute-start.2
  124.4 2.1 collective-permute-start.4
  130.5 7.8 %collective-permute-done.1 = bf16[512,512]{1,0:T(8,128)(2,1)} collective-permute-done((bf16[512,512]{1,0:T(8,128)(2,1)S(1)}, bf16[512,512]{1,0:T(8,128)(2,1)}, u32[]{:S(2)}, u32[]{:S(2)}) %collective-permute-start.1) | collective-permute-done | bytes 524320 | tf_op jit(solution)/shard_map/ppermute | solution.py:16
  140.7 20.1 %collective-permute-done.2 = bf16[512,512]{1,0:T(8,128)(2,1)} collective-permute-done((bf16[512,512]{1,0:T(8,128)(2,1)S(1)}, bf16[512,512]{1,0:T(8,128)(2,1)}, u32[]{:S(2)}, u32[]{:S(2)}) %collective-permute-start.2) | collective-permute-done | bytes 524320 | tf_op jit(solution)/shard_map/ppermute | solution.py:16
  163.3 1.8 collective-permute-done.3
  165.1 27.7 %collective-permute-done.4 = bf16[512,512]{1,0:T(8,128)(2,1)} collective-permute-done((bf16[512,512]{1,0:T(8,128)(2,1)S(1)}, bf16[512,512]{1,0:T(8,128)(2,1)}, u32[]{:S(2)}, u32[]{:S(2)}) %collective-permute-start.4) | collective-permute-done | bytes 524320 | tf_op jit(solution)/shard_map/ppermute | solution.py:16
  193.9 10.0 %collective-permute-done.6 = bf16[512,512]{1,0:T(8,128)(2,1)S(1)} collective-permute-done((bf16[512,512]{1,0:T(8,128)(2,1)S(1)}, bf16[512,512]{1,0:T(8,128)(2,1)S(1)}, u32[]{:S(2)}, u32[]{:S(2)}) %collective-permute-start.6) | collective-permute-done | bytes 524320 | tf_op jit(solution)/shard_map/ppermute | solution.py:16
  204.0 1.7 fusion.33
  205.7 136.0 %while.13 = (s32[]{:T(128)}, bf16[12,512,128]{1,2,0:T(8,128)(2,1)}, s32[4608]{0:T(1024)S(1)}, s32[512]{0:T(512)S(1)}, s32[12]{0:T(128)S(1)}, /*index=5*/bf16[512...) while((s32[]{:T(128)}, bf16[12,512,128]{1,2,0:T(8,128)(2,1)}, ...), condition=%wide.region_3.4_spmd.clone, body=%wide.region_0.3_spmd.clone.sunk | while | flops 1238700544 | bytes 31533952 | solution.py:88
  208.8 4.3 fusion.42
  220.1 4.3 fusion.42
  225.9 1.7 fusion.44
  231.5 4.3 fusion.42
  237.2 1.7 fusion.44
  242.8 4.3 fusion.42
  254.1 4.3 fusion.42
  265.5 4.3 fusion.42
  276.8 4.3 fusion.42
  288.2 4.3 fusion.42
  299.5 4.3 fusion.42
  310.8 4.3 fusion.42
  316.6 1.7 fusion.44
  322.2 4.3 fusion.42
  333.5 4.3 fusion.42
  341.7 27.4 %convolution_convert_fusion = bf16[512,12288]{1,0:T(8,128)(2,1)} fusion(bf16[512,1536]{0,1:T(8,128)(2,1)} %bitcast.36, bf16[1536,12288]{1,0:T(8,128)(2,1)} %all-gather.2.cloned.1.call-done), kind=kOutput, calls=%fused_computation.18 | convolution fusion | flops 19333644288 | bytes 51904512 | tf_op jit(solution)/shard_map/dot_general | solution.py:90
  369.2 217.1 %reduce-scatter.2.cloned.1.call-done = bf16[512,3072]{1,0:T(8,128)(2,1)} async-done(((bf16[512,12288]{1,0:T(8,128)(2,1)}), bf16[512,3072]{1,0:T(8,128)(2,1)}) %reduce-scatter.2.cloned.1.call-update) | async-done | bytes 3145744 | tf_op jit(solution)/shard_map/reduce_scatter | solution.py:95
  (127 shorter events, 65.3 us)
Async XLA Ops:
  6.5 0.7 copy-start.4
  6.5 1.0 copy-start.1
  6.5 1.5 copy-start
  6.5 1.5 copy-start.2
  6.5 335.2 %all-gather.2.cloned.1.call-start = ((), (), s32[]{:S(2)}) async-start(), calls=%async_computation.2 | async-start | bytes 42467328 | tf_op jit(solution)/shard_map/all_gather | solution.py:92
  14.9 95.4 %all-to-all-start = ((bf16[8,128,2048]{2,1,0:T(8,128)(2,1)}), bf16[8,128,2048]{2,1,0:T(8,128)(2,1)}, u32[]{:S(2)}, u32[]{:S(2)}) async-start(bf16[8,128,2048]{2,1,0:T(8,128)(2,1)} %copy.14), calls=%async_computation | async-start | bytes 8388608 | tf_op jit(solution)/shard_map/all_to_all | solution.py:50
  20.1 566.3 %reduce-scatter.2.cloned.1.call-start = ((), (), s32[]{:S(2)}) async-start(), calls=%async_computation.3 | async-start | bytes 15728640 | tf_op jit(solution)/shard_map/reduce_scatter | solution.py:95
  20.3 106.2 %copy-start.3 = (s32[4096]{0:T(1024)S(1)}, s32[4096]{0:T(1024)}, u32[]{:S(2)}) copy-start(s32[4096]{0:T(1024)} %param.11) | copy-start | bytes 49156
  116.8 11.1 %collective-permute-start = (bf16[512,512]{1,0:T(8,128)(2,1)S(1)}, bf16[512,512]{1,0:T(8,128)(2,1)}, u32[]{:S(2)}, u32[]{:S(2)}) collective-permute-start(bf16[512,512]{1,0:T(8,128)(2,1)S(1)} %slice.29), channel_id=1, source_target_pairs={} | collective-permute-start | bytes 1572872 | tf_op jit(solution)/shard_map/ppermute | solution.py:16
  118.2 20.0 %collective-permute-start.1 = (bf16[512,512]{1,0:T(8,128)(2,1)S(1)}, bf16[512,512]{1,0:T(8,128)(2,1)}, u32[]{:S(2)}, u32[]{:S(2)}) collective-permute-start(bf16[512,512]{1,0:T(8,128)(2,1)S(1)} %slice.29), channel_id=1, source_target_pairs={{0,28},{1,29},{2,30},{3,31}} | collective-permute-start | bytes 1572872 | tf_op jit(solution)/shard_map/ppermute | solution.py:16
  120.4 40.3 %collective-permute-start.2 = (bf16[512,512]{1,0:T(8,128)(2,1)S(1)}, bf16[512,512]{1,0:T(8,128)(2,1)}, u32[]{:S(2)}, u32[]{:S(2)}) collective-permute-start(bf16[512,512]{1,0:T(8,128)(2,1)S(1)} %slice.29), channel_id=1, source_target_pairs={{0,24},{4,28},{1,25},{5,29},{2,26},{6,30},{3,27},{7,31}} | collective-permute-start | bytes 1572872 | tf_op jit(solution)/shard_map/ppermute | solution.py:16
  123.1 42.0 %collective-permute-start.3 = (bf16[512,512]{1,0:T(8,128)(2,1)S(1)}, bf16[512,512]{1,0:T(8,128)(2,1)S(1)}, u32[]{:S(2)}, u32[]{:S(2)}) collective-permute-start(bf16[512,512]{1,0:T(8,128)(2,1)S(1)} %slice.29), channel_id=1, source_target_pairs={{0,20},{4,24},{8,28},{1,21},{5,25},{9,29},{2,22},{6,26},{10,30},{3... | collective-permute-start | bytes 1572872 | tf_op jit(solution)/shard_map/ppermute | solution.py:16
  124.4 68.4 %collective-permute-start.4 = (bf16[512,512]{1,0:T(8,128)(2,1)S(1)}, bf16[512,512]{1,0:T(8,128)(2,1)}, u32[]{:S(2)}, u32[]{:S(2)}) collective-permute-start(bf16[512,512]{1,0:T(8,128)(2,1)S(1)} %slice.29), channel_id=1, source_target_pairs={{0,16},{4,20},{8,24},{12,28},{1,17},{5,21},{9,25},{13,29},{2,18},{... | collective-permute-start | bytes 1572872 | tf_op jit(solution)/shard_map/ppermute | solution.py:16
  127.9 65.9 %collective-permute-start.5 = (bf16[512,512]{1,0:T(8,128)(2,1)S(1)}, bf16[512,512]{1,0:T(8,128)(2,1)S(1)}, u32[]{:S(2)}, u32[]{:S(2)}) collective-permute-start(bf16[512,512]{1,0:T(8,128)(2,1)S(1)} %slice.29), channel_id=1, source_target_pairs={{0,12},{4,16},{8,20},{12,24},{16,28},{1,13},{5,17},{9,21},{13,25},... | collective-permute-start | bytes 1572872 | tf_op jit(solution)/shard_map/ppermute | solution.py:16
  138.3 65.6 %collective-permute-start.6 = (bf16[512,512]{1,0:T(8,128)(2,1)S(1)}, bf16[512,512]{1,0:T(8,128)(2,1)S(1)}, u32[]{:S(2)}, u32[]{:S(2)}) collective-permute-start(bf16[512,512]{1,0:T(8,128)(2,1)S(1)} %slice.29), channel_id=1, source_target_pairs={{0,8},{4,12},{8,16},{12,20},{16,24},{20,28},{1,9},{5,13},{9,17},{1... | collective-permute-start | bytes 1572872 | tf_op jit(solution)/shard_map/ppermute | solution.py:16
  160.7 43.2 %collective-permute-start.7 = (bf16[512,512]{1,0:T(8,128)(2,1)S(1)}, bf16[512,512]{1,0:T(8,128)(2,1)S(1)}, u32[]{:S(2)}, u32[]{:S(2)}) collective-permute-start(bf16[512,512]{1,0:T(8,128)(2,1)S(1)} %slice.29), channel_id=1, source_target_pairs={{0,4},{4,8},{8,12},{12,16},{16,20},{20,24},{24,28},{1,5},{5,9},{9,... | collective-permute-start | bytes 1572872 | tf_op jit(solution)/shard_map/ppermute | solution.py:16
Sparse Core Ops, SparseCore 0:
  9.3 262.2 all-gather.1
  369.3 216.9 reduce-scatter.1
where the time goes:
time: 594 us; the launch traced here: 593 us
  waiting for transfers between devices  375 us (63%)
  matrix products  107 us (18%)
  local copies, waits for them, and re-layouts  30.7 us (5%)
  loops' own time  29.9 us (5%)
  starting transfers between devices  19 us (3%)
  other arithmetic  17.5 us (3%)
  between operations  13.6 us (2%)
    reduce_scatter x1, waiting for transfers between devices, shards(): lax.psum_scatter(terms.astype(jnp.bfloat16), 'tp', scatter_dimension=1, t...  217 us
    all_to_all x1, waiting for transfers between devices, shards(): lax.all_to_all(outgoing, 'seq', split_axis=0, concat_axis=0, tiled=True)  90 us
    ppermute x8, waiting for transfers between devices, passed_along(): return lax.ppermute(block, axis, route)  67.2 us
    dot_general x12, matrix products, attend_head(): lax.dot_general(q_rows, k_rows, (((1,), (1,)), ((), ())), preferred_eleme...  51.9 us
    another operation x1, loops' own time, shards(): per_head = lax.map(one_head, jnp.arange(heads_here, dtype=jnp.int32))  29.9 us
    dot_general x1, matrix products, shards(): jnp.dot(attended, lax.all_gather(out_weight, 'seq', axis=1, tiled=True),...  27.4 us
    dot_general x12, matrix products, attend_head(): jnp.dot(weights, v_rows, preferred_element_type=jnp.float32)  20.3 us
    reduce_sum x12, other arithmetic, attend_head(): weights = (expo / jnp.sum(expo, axis=1, keepdims=True)).astype(jnp.bfloat16)  17.1 us
  transfers between devices with their start and end apart: 11, of which 7 were waited for; matrix products, arithmetic and copies ran while one was open for 21% of the time, Pallas kernels for 0%

commit v1 on v0

v1 whole, which is shorter than its diff:
```python
import functools
import math

import jax
import jax.numpy as jnp
from jax import lax
from jax.experimental import pallas as pl
from jax.experimental.pallas import tpu as pltpu
from jax.sharding import PartitionSpec as P

HEAD_DIM = 128
WINDOW = 4096
BLOCK = 128
KEY_TILE = 512
MASKED = -1e30
SCALE = math.log2(math.e) / math.sqrt(HEAD_DIM)


def attention_kernel(group, kv_heads, n_kv, place, low, rows_at, q_ref, qseg_ref, seg_ref, *refs):
    kv_refs, out_ref, packed_kv = refs[:n_kv], refs[n_kv], refs[n_kv + 1]
    step = pl.program_id(0)
    kv_rows = kv_refs[0].shape[0]

    @pl.when(step == 0)
    def _():
        def move(block, _):
            row = rows_at[block]
            for i, kv_ref in enumerate(kv_refs):

                @pl.when((row >= i * kv_rows) & (row < (i + 1) * kv_rows))
                def _(i=i, kv_ref=kv_ref):
                    at = pl.multiple_of(row - i * kv_rows, BLOCK)
                    packed_kv[pl.ds(pl.multiple_of(block * BLOCK, BLOCK), BLOCK), :] = kv_ref[pl.ds(at, BLOCK), :]

            return 0

        lax.fori_loop(0, rows_at.shape[0], move, 0)

    first = place[step] * BLOCK
    q_pos = first + lax.broadcasted_iota(jnp.int32, (BLOCK, KEY_TILE), 0)
    q_seg = qseg_ref[...]
    lo_tile = low[step] // KEY_TILE
    hi_tile = (first + BLOCK - 1) // KEY_TILE + 1
    kv_cols = kv_heads * HEAD_DIM

    for kv_head in range(kv_heads):
        q = jnp.concatenate(
            [q_ref[:, (kv_head * group + h) * HEAD_DIM : (kv_head * group + h + 1) * HEAD_DIM] for h in range(group)],
            axis=0,
        )
        q = (q.astype(jnp.float32) * SCALE).astype(jnp.bfloat16)

        def tile(t, carry, q=q, kv_head=kv_head):
            top, total, acc = carry
            rows = pl.ds(pl.multiple_of(t * KEY_TILE, KEY_TILE), KEY_TILE)
            keys = packed_kv[rows, kv_head * HEAD_DIM : (kv_head + 1) * HEAD_DIM]
            values = packed_kv[rows, kv_cols + kv_head * HEAD_DIM : kv_cols + (kv_head + 1) * HEAD_DIM]
            k_pos = t * KEY_TILE + lax.broadcasted_iota(jnp.int32, (BLOCK, KEY_TILE), 1)
            kept = (k_pos <= q_pos) & (k_pos > q_pos - WINDOW) & (seg_ref[:, rows] == q_seg)
            scores = lax.dot_general(q, keys, (((1,), (1,)), ((), ())), preferred_element_type=jnp.float32)
            scores = jnp.where(kept[None], scores.reshape(group, BLOCK, KEY_TILE), MASKED)
            scores = scores.reshape(group * BLOCK, KEY_TILE)
            new_top = jnp.maximum(top, jnp.max(scores, axis=1, keepdims=True))
            expo = jnp.exp2(scores - new_top)
            keep = jnp.exp2(top - new_top)
            total = total * keep + jnp.sum(expo, axis=1, keepdims=True)
            acc = acc * keep + jnp.dot(expo.astype(jnp.bfloat16), values, preferred_element_type=jnp.float32)
            return new_top, total, acc

        rows = group * BLOCK
        start = (
            jnp.full((rows, 1), MASKED, jnp.float32),
            jnp.zeros((rows, 1), jnp.float32),
            jnp.zeros((rows, HEAD_DIM), jnp.float32),
        )
        _, total, acc = lax.fori_loop(lo_tile, hi_tile, tile, start)
        heads = (acc / total).astype(jnp.bfloat16)
        for h in range(group):
            at = (kv_head * group + h) * HEAD_DIM
            out_ref[:, at : at + HEAD_DIM] = heads[h * BLOCK : (h + 1) * BLOCK]


def attend(q, kv, rows_at, place, segment_ids, first=0):
    blocks = place.shape[0]
    tokens = segment_ids.shape[0]
    kv_heads = kv[0].shape[1] // (2 * HEAD_DIM)
    group = q.shape[1] // HEAD_DIM // kv_heads
    q_seg = segment_ids.reshape(-1, BLOCK)[place]
    doc_first = jnp.sum((segment_ids[None, :] < q_seg[:, :1]).astype(jnp.int32), axis=1)
    low = jnp.maximum(doc_first, place * BLOCK - (WINDOW - 1))
    grid = pltpu.PrefetchScalarGridSpec(
        num_scalar_prefetch=3,
        grid=(blocks,),
        in_specs=[
            pl.BlockSpec((BLOCK, q.shape[1]), lambda i, *_: (first + i, 0)),
            pl.BlockSpec((BLOCK, 1), lambda i, *_: (i, 0)),
            pl.BlockSpec((1, tokens), lambda i, *_: (0, 0)),
        ]
        + [pl.BlockSpec(part.shape, lambda i, *_: (0, 0)) for part in kv],
        out_specs=pl.BlockSpec((BLOCK, q.shape[1]), lambda i, *_: (i, 0)),
        scratch_shapes=[pltpu.VMEM((tokens, kv[0].shape[1]), jnp.bfloat16)],
    )
    rows = blocks * BLOCK
    return pl.pallas_call(
        functools.partial(attention_kernel, group, kv_heads, len(kv)),
        grid_spec=grid,
        out_shape=jax.ShapeDtypeStruct((rows, q.shape[1]), jnp.bfloat16),
        compiler_params=pltpu.CompilerParams(vmem_limit_bytes=48 << 20),
        cost_estimate=pl.CostEstimate(
            flops=4 * rows * q.shape[1] * tokens // 2,
            bytes_accessed=4 * rows * q.shape[1] + 2 * tokens * kv[0].shape[1],
            transcendentals=rows * (q.shape[1] // HEAD_DIM) * tokens // 2,
        ),
        name="attend",
    )(place, low, rows_at, q, q_seg.reshape(-1, 1), segment_ids.reshape(1, -1), *kv)


def product_kernel(layout, slots, *refs):
    del slots
    out_ref = refs[-1]
    row = 0
    for h, w, adds in layout:
        total = jnp.dot(refs[h][...], refs[w][...], preferred_element_type=jnp.float32)
        for a in adds:
            total = total + refs[a][...].astype(jnp.float32)
        rows = total.shape[0]
        out_ref[row : row + rows, :] = total.astype(out_ref.dtype)
        row += rows


def product(parts, weight, slots, adds=None, tile=384, first=0, tiles=None):
    depth, cols = weight.shape[1:]
    per_group = cols // tile
    tiles = tiles or per_group
    operands = [weight]
    in_specs = [pl.BlockSpec((None, depth, tile), lambda g, j, s: (s[g], 0, first + j))]
    layout = []
    for p, h in enumerate(parts):
        rows = h.shape[0]
        operands.append(h)
        in_specs.append(pl.BlockSpec((rows, depth), lambda g, j, s: (0, 0)))
        at, more = len(operands) - 1, []
        for a, r, slotted in adds[p] if adds else ():
            operands.append(a)
            if slotted:
                in_specs.append(pl.BlockSpec((rows, tile), lambda g, j, s, r=r: (r, s[g] * per_group + first + j)))
            else:
                in_specs.append(pl.BlockSpec((rows, tile), lambda g, j, s, r=r: (r, g * tiles + j)))
            more.append(len(operands) - 1)
        layout.append((at, 0, more))
    rows = sum(h.shape[0] for h in parts)
    groups = slots.shape[0]
    return pl.pallas_call(
        functools.partial(product_kernel, layout),
        grid_spec=pltpu.PrefetchScalarGridSpec(
            num_scalar_prefetch=1,
            grid=(groups, tiles),
            in_specs=in_specs,
            out_specs=pl.BlockSpec((rows, tile), lambda g, j, s: (0, g * tiles + j)),
        ),
        out_shape=jax.ShapeDtypeStruct((rows, groups * tiles * tile), jnp.bfloat16),
        compiler_params=pltpu.CompilerParams(vmem_limit_bytes=40 << 20),
        cost_estimate=pl.CostEstimate(
            flops=2 * rows * depth * groups * tiles * tile,
            bytes_accessed=2 * depth * (rows + groups * tiles * tile) + 4 * rows * groups * tiles * tile,
            transcendentals=0,
        ),
        name="product",
    )(slots, *operands)


def pick_kernel(pools, source, *refs):
    outs = refs[pools:]
    per_out = outs[0].shape[0] // BLOCK
    for i in range(source.shape[0]):
        row = source[i] * BLOCK
        out = outs[i // per_out]
        to = slice(i % per_out * BLOCK, (i % per_out + 1) * BLOCK)
        low = 0
        for pool in refs[:pools]:

            @pl.when((row >= low) & (row < low + pool.shape[0]))
            def _(pool=pool, row=row, out=out, to=to, low=low):
                out[to, :] = pool[pl.ds(pl.multiple_of(row - low, BLOCK), BLOCK), :]

            low += pool.shape[0]


def pick_blocks(pools, cols, source, outs):
    rows = source.shape[0] * BLOCK // outs
    size = 2 * cols * (sum(p.shape[0] for p, _ in pools) + rows * outs)
    return pl.pallas_call(
        functools.partial(pick_kernel, len(pools)),
        grid_spec=pltpu.PrefetchScalarGridSpec(
            num_scalar_prefetch=1,
            grid=(1,),
            in_specs=[pl.BlockSpec((p.shape[0], cols), lambda i, s, g=g: (0, g)) for p, g in pools],
            out_specs=[pl.BlockSpec((rows, cols), lambda i, s: (0, 0))] * outs,
        ),
        out_shape=[jax.ShapeDtypeStruct((rows, cols), jnp.bfloat16)] * outs,
        compiler_params=pltpu.CompilerParams(vmem_limit_bytes=40 << 20),
        cost_estimate=pl.CostEstimate(flops=0, bytes_accessed=size, transcendentals=0),
        name="pick_blocks",
    )(source, *[p for p, _ in pools])


def sources_of(packing, per_shard):
    blocks = packing.shape[0]
    target = packing[:, 0] * per_shard + packing[:, 1]
    at = jnp.arange(blocks, dtype=jnp.int32)
    return target, jnp.sum(jnp.where(target[None, :] == at[:, None], at[None, :], 0), axis=1)


def plain_plan(queries, keys, values, segment_ids, packing, out_weight):
    tok_rows = queries.shape[0]
    per_shard = tok_rows // BLOCK
    me = lax.axis_index("seq")
    target, source = sources_of(packing, per_shard)
    place = lax.dynamic_slice_in_dim(target, me * per_shard, per_shard, 0)
    kv = lax.all_gather(jnp.concatenate([keys, values], axis=1), "seq", axis=0, tiled=True)
    heads = attend(queries, [kv], source * BLOCK, place, segment_ids)
    heads = lax.all_gather(heads, "seq", axis=0, tiled=True)
    own = lax.dynamic_slice_in_dim(source, me * per_shard, per_shard, 0)
    heads = heads.reshape(-1, BLOCK, heads.shape[1])[own].reshape(tok_rows, -1)
    weight = lax.all_gather(out_weight, "seq", axis=1, tiled=True)
    terms = jnp.dot(heads, weight, preferred_element_type=jnp.float32).astype(jnp.bfloat16)
    return lax.psum_scatter(terms, "tp", scatter_dimension=1, tiled=True)


def after(array, *others):
    return lax.optimization_barrier((array, *others))[0]


def paired_plan(queries, keys, values, segment_ids, packing, out_weight):
    tok_rows, q_cols = queries.shape
    per_shard = tok_rows // BLOCK
    quarter = out_weight.shape[1] // 2
    half = quarter // 2
    me, z = lax.axis_index("seq"), lax.axis_index("tp")
    chip, core = me // 2, me % 2
    x, pair = chip % 2, z // 2
    target, source = sources_of(packing, per_shard)
    place = lax.dynamic_slice_in_dim(target, me * per_shard, per_shard, 0)

    def across(array, mask):
        return lax.ppermute(array, "seq", [(i, i ^ mask) for i in range(8)])

    def along(array, *route):
        return lax.ppermute(array, "tp", route)

    kv = jnp.concatenate([keys, values], axis=1)
    kv_x, kv_y, kv_d = across(kv, 2), across(kv, 4), across(kv, 6)
    pieces = [lax.dynamic_slice_in_dim(out_weight, (x ^ flip) * quarter, quarter, 1) for flip in range(2)]
    kv_own = jnp.concatenate([kv, after(kv_x, *pieces), kv_y, kv_d], axis=0)
    kv_other = across(kv_own, 1)

    def row_of(block):
        relative = (block // per_shard) ^ me
        return ((relative >> 1) + 4 * (relative & 1)) * tok_rows + block % per_shard * BLOCK

    weights = []
    for flip, piece in enumerate(pieces):
        route = []
        for s in range(8):
            sy, sx, sa = s // 4, s // 2 % 2, s % 2
            d = 4 * sa + 2 * (sx ^ flip) + sy
            if s != d:
                route.append((s, d))
        weights.append(lax.ppermute(after(piece, kv_x, kv_y, kv_d), "seq", route))
    weights[0] = jnp.where(core == chip // 2, pieces[0], weights[0])

    heads = attend(queries, [kv_own, kv_other], row_of(source), place, segment_ids)
    mine = [heads, across(heads, 2), across(heads, 4)]

    weights = [(own, across(after(own, heads), 1)) for own in weights]

    here = core == pair
    near = jnp.stack([jnp.where(here, own, other) for own, other in weights])
    far = [jnp.where(here, other, own)[None] for own, other in weights]
    both = jnp.concatenate(far, axis=0)
    first, flips = jnp.zeros((1,), jnp.int32), jnp.arange(2, dtype=jnp.int32)

    def add(a, b):
        return (a.astype(jnp.float32) + b.astype(jnp.float32)).astype(jnp.bfloat16)

    shares = [(0, far[0]), (0, far[1]), (1, both), (2, both), (3, both)]
    inward, sums, arrived = [], [], []
    for i, (r, w) in enumerate(shares):
        if i == 2:
            mine.append(across(after(heads, shares[1], mine[1], mine[2]), 6))
        rows = mine[r]
        if i == 1:
            rows = after(rows, shares[0])
        elif i:
            rows = after(rows, shares[i - 1], sums[i - 2], *arrived[: i - 2])
        shares[i] = product([rows], w, first if i < 2 else flips)
        inward.append(along(shares[i], (0, 1), (3, 2)))
        sums.append(add(shares[i], inward[i]))
        arrived.append(along(sums[i], (1, 2), (2, 1)))

    own_slot = ((z & 1) ^ x).astype(jnp.int32)[None]

    near_adds = [jnp.concatenate(arrived[:2], axis=1), *arrived[2:]]

    def swap(r, first=0, tiles=2):
        share = product([mine[r]], near, 1 - own_slot, [[(near_adds[r], 0, True)]], half, first, tiles)
        return along(share, (0, 1), (1, 0), (2, 3), (3, 2))

    def total(parts, swapped, first=0, tiles=2):
        adds = [[(near_adds[r], 0, True), (some, 0, False)] for r, some in zip(parts, swapped)]
        return product([mine[r] for r in parts], near, own_slot, adds, half, first, tiles)

    early = [swap(r) for r in range(3)]
    late = [swap(3, h, 1) for h in range(2)]
    done = total((0, 1, 2), early)
    done = [done, across(done, 1)]

    picks = []
    for r in range(4):
        blocks = lax.dynamic_slice_in_dim(source, (me ^ (2 * r)) * per_shard, per_shard, 0)
        picks.append(row_of(blocks) // BLOCK)
    picks = jnp.concatenate(picks)
    result = jnp.zeros((tok_rows, 4 * quarter), jnp.bfloat16)
    for h in range(2):
        last = total((3,), [late[h]], h, 1)
        rows = pick_blocks([(done[0], h), (last, 0), (done[1], h), (across(last, 1), 0)], half, picks, 4)
        for r in range(4):
            some = across(rows[r], 2 * r) if r else rows[r]
            result = lax.dynamic_update_slice_in_dim(result, some, (chip ^ r) * quarter + h * half, 1)
    return result


def solution(mesh):
    in_specs = (P("seq", "tp"), P("seq", "tp"), P("seq", "tp"), P(), P(), P("tp", "seq"))
    out_specs = P("seq", "tp")
    paired = mesh.shape["seq"] == 8 and mesh.shape["tp"] == 4
    shards = paired_plan if paired else plain_plan
    return jax.shard_map(shards, mesh=mesh, in_specs=in_specs, out_specs=out_specs, check_vma=False)
```

time: 594 us -> 382 us (0.64)
  waiting for transfers between devices: 375 us -> 173 us
  matrix products: 107 us -> 0 us
  Pallas kernels: 0 us -> 74.5 us
  starting transfers between devices: 19 us -> 87 us
  loops' own time: 29.9 us -> 0 us
  between operations: 13.6 us -> 0.59 us
  local copies, waits for them, and re-layouts: 30.7 us -> 21.7 us
  other arithmetic: 17.5 us -> 24.5 us
    reduce_scatter x1 -> x0, waiting for transfers between devices: 217 us -> none  [shards(): lax.psum_scatter(terms.astype(jnp.bfloat16), 'tp', scatter_dimension=1, t...]
    dot_general x28 -> x0, matrix products: 107 us -> none  [the longest x12 51.9 us: attend_head(): lax.dot_general(q_rows, k_rows, (((1,), (1,)), ((), ())), preferred_eleme...]
    ppermute x8 -> x35, waiting for transfers between devices: 67.2 us -> 173 us  [the longest x15 123 us: along(): return lax.ppermute(array, 'tp', route)]
    all_to_all x1 -> x0, waiting for transfers between devices: 90 us -> none  [shards(): lax.all_to_all(outgoing, 'seq', split_axis=0, concat_axis=0, tiled=True)]
    pallas_call x0 -> x16, Pallas kernels: none -> 74.5 us  [the longest x13 43.4 us: product(): pl.pallas_call(functools.partial(product_kernel, layout), grid_spec=pltpu...]
    ppermute x8 -> x35, starting transfers between devices: 13.8 us -> 87 us  [the longest x15 49 us: along(): return lax.ppermute(array, 'tp', route)]
    another operation x1 -> x0, loops' own time: 29.9 us -> none  [shards(): per_head = lax.map(one_head, jnp.arange(heads_here, dtype=jnp.int32))]
    reduce_sum x12 -> x2, other arithmetic: 17.1 us -> 0.33 us  [the longest x1 0.22 us: attend(): jnp.sum((segment_ids[None, :] < q_seg[:, :1]).astype(jnp.int32), axis=1)]
  transfers between devices with their start and end apart: 11 -> 35, of which waited for: 7 -> 19; matrix products, arithmetic and copies ran while one was open for 21% -> 8% of each run, Pallas kernels for 0% -> 20%
where the time goes in v1:
time: 382 us; the launch traced here: 381 us
  waiting for transfers between devices  173 us (45%)
  starting transfers between devices  87 us (23%)
  Pallas kernels  74.5 us (20%)
  other arithmetic  24.5 us (6%)
  local copies, waits for them, and re-layouts  21.7 us (6%)
    ppermute x15, waiting for transfers between devices, along(): return lax.ppermute(array, 'tp', route)  123 us
    ppermute x15, starting transfers between devices, along(): return lax.ppermute(array, 'tp', route)  49 us
    ppermute x18, waiting for transfers between devices, across(): return lax.ppermute(array, 'seq', [(i, i ^ mask) for i in range(8)])  49 us
    pallas_call x13, Pallas kernels, product(): pl.pallas_call(functools.partial(product_kernel, layout), grid_spec=pltpu...  43.4 us
    ppermute x18, starting transfers between devices, across(): return lax.ppermute(array, 'seq', [(i, i ^ mask) for i in range(8)])  35.3 us
    pallas_call x1, Pallas kernels, attend(): pl.pallas_call(functools.partial(attention_kernel, group, kv_heads, len(k...  25.5 us
    unnamed x50, local copies, waits for them, and re-layouts  11.3 us
    broadcast_in_dim x2, other arithmetic, paired_plan(): far = [jnp.where(here, other, own)[None] for own, other in weights]  8.16 us
  transfers between devices with their start and end apart: 35, of which 19 were waited for; matrix products, arithmetic and copies ran while one was open for 8% of the time, Pallas kernels for 20%

profile of v1, /device:TPU:0, one launch (start us, length us, event | category | flops | bytes accessed | tf_op | source)
XLA Modules:
  0.0 381.3 jit_solution(600740463611159751)
XLA Ops:
  6.5 4.8 %constant_dynamic-slice_fusion.2 = (bf16[1536,768]{1,0:T(8,128)(2,1)}, bf16[1536,768]{1,0:T(8,128)(2,1)}) fusion(bf16[1536,1536]{1,0:T(8,128)(2,1)} %param.11, s32[]{:T(128)S(6)} %select_n.176, s32[]{:T(128)S(6)} %select_n.181), kind=kLoop, calls=%fused_computation.33 | loop fusion | bytes 9437192 | tf_op jit(solution)/shard_map/dynamic_slice | solution.py:253
  11.3 6.4 %collective-permute-done = bf16[512,512]{1,0:T(8,128)(2,1)S(1)} collective-permute-done((bf16[512,512]{1,0:T(8,128)(2,1)S(1)}, bf16[512,512]{1,0:T(8,128)(2,1)S(1)}, u32[]{:S(2)}, u32[]{:S(2)}) %collective-permute-start) | collective-permute-done | bytes 524320 | tf_op jit(solution)/shard_map/ppermute | solution.py:246
  17.7 11.9 %collective-permute-done.1 = bf16[512,512]{1,0:T(8,128)(2,1)S(1)} collective-permute-done((bf16[512,512]{1,0:T(8,128)(2,1)S(1)}, bf16[512,512]{1,0:T(8,128)(2,1)S(1)}, u32[]{:S(2)}, u32[]{:S(2)}) %collective-permute-start.1) | collective-permute-done | bytes 524320 | tf_op jit(solution)/shard_map/ppermute | solution.py:246
  40.1 25.5 %attend.1.refs_1_ = bf16[512,1536]{1,0:T(8,128)(2,1)S(1)} custom-call(s32[4]{0:T(128)S(1)} %get-tuple-element.42.place, s32[4]{0:T(128)S(1)} %add_maximum_fusion.low, s32[32]{0:T(128)S(1)} %fusion.9.rows_at, bf16[512,1536]{1,0:T(8,128)(2,1)S(1)} %copy-done.14, s32[512,1]{1,0:T(8,128)S(1)} %copy.8.qseg_ref, s32[1,4096]{1,0:T(1,128)S(1)} %bitcast.20, ...), custom_call_target="tpu_custom_call" | custom-call | flops 6442450944 | bytes 7340032 | tf_op jit(solution)/shard_map/attend/pallas_call | solution.py:104
  65.6 3.9 %broadcast_select_fusion = bf16[1536,768]{1,0:T(8,128)(2,1)} fusion(bf16[1536,768]{1,0:T(8,128)(2,1)} %get-tuple-element.23, bf16[1536,768]{1,0:T(8,128)(2,1)} %collective-permute-done.3, pred[]{:T(512)S(6)} %eq.33), kind=kLoop, calls=%fused_computation.10 | loop fusion | flops 1179648 | bytes 7077889 | tf_op jit(solution)/shard_map/jit(_where)/select_n | solution.py:270
  69.5 19.9 %collective-permute-start.5 = (bf16[1536,768]{1,0:T(8,128)(2,1)}, bf16[1536,768]{1,0:T(8,128)(2,1)}, u32[]{:S(2)}, u32[]{:S(2)}) collective-permute-start(bf16[1536,768]{1,0:T(8,128)(2,1)} %broadcast_select_fusion), channel_id=1, source_target_pairs={{0,4},{4,0},{8,12},{12,8},{16,20},{20,16},{24,28},{28,24},{1,5},{5... | collective-permute-start | bytes 7077896 | tf_op jit(solution)/shard_map/ppermute | solution.py:246
  93.9 4.1 %select_bitcast_fusion.1 = (bf16[1,1536,768]{2,1,0:T(8,128)(2,1)S(1)}, bf16[1,1536,768]{2,1,0:T(8,128)(2,1)}) fusion(bf16[1536,768]{1,0:T(8,128)(2,1)} %collective-permute-done.5, bf16[1536,768]{1,0:T(8,128)(2,1)} %broadcast_select_fusion, pred[]{:T(512)S(6)} %eq.32), kind=kLoop, calls=%fused_computation.7 | loop fusion | flops 2359296 | bytes 9437185 | tf_op jit(solution)/shard_map/broadcast_in_dim | solution.py:279
  100.3 3.5 collective-permute-start.8
  103.9 4.1 %select_bitcast_fusion = (bf16[1,1536,768]{2,1,0:T(8,128)(2,1)S(1)}, bf16[1,1536,768]{2,1,0:T(8,128)(2,1)}) fusion(bf16[1536,768]{1,0:T(8,128)(2,1)} %collective-permute-done.7, bf16[1536,768]{1,0:T(8,128)(2,1)} %collective-permute-done.6, pred[]{:T(512)S(6)} %eq.32), kind=kLoop, calls=%fused_computation.6 | loop fusion | flops 2359296 | bytes 9437185 | tf_op jit(solution)/shard_map/broadcast_in_dim | solution.py:279
  111.6 10.1 %collective-permute-done.8 = bf16[512,768]{1,0:T(8,128)(2,1)S(1)} collective-permute-done((bf16[512,768]{1,0:T(8,128)(2,1)S(1)}, bf16[512,768]{1,0:T(8,128)(2,1)S(1)}, u32[]{:S(2)}, u32[]{:S(2)}) %collective-permute-start.8) | collective-permute-done | bytes 786464 | tf_op jit(solution)/shard_map/ppermute | solution.py:249
  123.1 4.5 %collective-permute-done.13.refs_1_.refs_4_ = bf16[512,1536]{1,0:T(8,128)(2,1)S(1)} collective-permute-done((bf16[512,1536]{1,0:T(8,128)(2,1)S(1)}, bf16[512,1536]{1,0:T(8,128)(2,1)S(1)}, u32[]{:S(2)}, u32[]{:S(2)}) %collective-permute-start.13) | collective-permute-done | bytes 1572896 | tf_op jit(solution)/shard_map/ppermute | solution.py:246
  127.6 5.2 %product.16 = bf16[512,1536]{1,0:T(8,128)(2,1)S(1)} custom-call(s32[2]{0:T(128)S(1)} %iota.14.slots, bf16[2,1536,768]{2,1,0:T(8,128)(2,1)S(1)} %pad_maximum_fusion.1.refs_0_, bf16[512,1536]{1,0:T(8,128)(2,1)S(1)} %collective-permute-done.13.refs_1_.refs_4_), custom_call_target="tpu_custom_call" | custom-call | flops 2415919104 | bytes 9437184 | tf_op jit(solution)/shard_map/product/pallas_call | solution.py:153
  132.8 3.6 collective-permute-start.14
  139.7 5.2 %product.18 = bf16[512,1536]{1,0:T(8,128)(2,1)S(1)} custom-call(s32[2]{0:T(128)S(1)} %iota.15.slots, bf16[2,1536,768]{2,1,0:T(8,128)(2,1)S(1)} %pad_maximum_fusion.1.refs_0_, bf16[512,1536]{1,0:T(8,128)(2,1)S(1)} %collective-permute-done.17.refs_1_.refs_7_), custom_call_target="tpu_custom_call" | custom-call | flops 2415919104 | bytes 9437184 | tf_op jit(solution)/shard_map/product/pallas_call | solution.py:153
  144.9 7.9 %collective-permute-start.18 = (bf16[512,1536]{1,0:T(8,128)(2,1)S(1)}, bf16[512,1536]{1,0:T(8,128)(2,1)S(1)}, u32[]{:S(2)}, u32[]{:S(2)}) collective-permute-start(bf16[512,1536]{1,0:T(8,128)(2,1)S(1)} %product.18), channel_id=1, source_target_pairs={{0,1},{3,2},{4,5},{7,6},{8,9},{11,10},{12,13},{15,14},{16,17},{19,... | collective-permute-start | bytes 4718600 | tf_op jit(solution)/shard_map/ppermute | solution.py:249
  154.8 17.4 %collective-permute-done.14 = bf16[512,1536]{1,0:T(8,128)(2,1)S(1)} collective-permute-done((bf16[512,1536]{1,0:T(8,128)(2,1)S(1)}, bf16[512,1536]{1,0:T(8,128)(2,1)S(1)}, u32[]{:S(2)}, u32[]{:S(2)}) %collective-permute-start.14) | collective-permute-done | bytes 1572896 | tf_op jit(solution)/shard_map/ppermute | solution.py:249
  175.7 29.7 %collective-permute-done.18 = bf16[512,1536]{1,0:T(8,128)(2,1)S(1)} collective-permute-done((bf16[512,1536]{1,0:T(8,128)(2,1)S(1)}, bf16[512,1536]{1,0:T(8,128)(2,1)S(1)}, u32[]{:S(2)}, u32[]{:S(2)}) %collective-permute-start.18) | collective-permute-done | bytes 1572896 | tf_op jit(solution)/shard_map/ppermute | solution.py:249
  208.9 5.9 %product.21 = bf16[512,1536]{1,0:T(8,128)(2,1)} custom-call(s32[2]{0:T(128)S(1)} %iota.16.slots, bf16[2,1536,768]{2,1,0:T(8,128)(2,1)S(1)} %pad_maximum_fusion.1.refs_0_, bf16[512,1536]{1,0:T(8,128)(2,1)S(1)} %collective-permute-done.21.refs_1_), custom_call_target="tpu_custom_call" | custom-call | flops 2415919104 | bytes 9437184 | tf_op jit(solution)/shard_map/product/pallas_call | solution.py:153
  214.7 7.4 %collective-permute-start.22 = (bf16[512,1536]{1,0:T(8,128)(2,1)}, bf16[512,1536]{1,0:T(8,128)(2,1)}, u32[]{:S(2)}, u32[]{:S(2)}) collective-permute-start(bf16[512,1536]{1,0:T(8,128)(2,1)} %product.21), channel_id=1, source_target_pairs={{0,1},{3,2},{4,5},{7,6},{8,9},{11,10},{12,13},{15,14},{16,17},{19,... | collective-permute-start | bytes 4718600 | tf_op jit(solution)/shard_map/ppermute | solution.py:249
  236.3 14.6 %collective-permute-start.20 = (bf16[512,768]{1,0:T(8,128)(2,1)S(1)}, bf16[512,768]{1,0:T(8,128)(2,1)S(1)}, u32[]{:S(2)}, u32[]{:S(2)}) collective-permute-start(bf16[512,768]{1,0:T(8,128)(2,1)S(1)} %product.19), channel_id=1, source_target_pairs={{0,1},{1,0},{2,3},{3,2},{4,5},{5,4},{6,7},{7,6},{8,9},{9,8},{10,11... | collective-permute-start | bytes 2359304 | tf_op jit(solution)/shard_map/ppermute | solution.py:249
  250.9 5.2 %collective-permute-done.22 = bf16[512,1536]{1,0:T(8,128)(2,1)} collective-permute-done((bf16[512,1536]{1,0:T(8,128)(2,1)}, bf16[512,1536]{1,0:T(8,128)(2,1)}, u32[]{:S(2)}, u32[]{:S(2)}) %collective-permute-start.22) | collective-permute-done | bytes 1572896 | tf_op jit(solution)/shard_map/ppermute | solution.py:249
  256.1 3.6 add_convert_fusion
  260.5 12.3 %collective-permute-done.12.refs_3_ = bf16[512,768]{1,0:T(8,128)(2,1)S(1)} collective-permute-done((bf16[512,768]{1,0:T(8,128)(2,1)S(1)}, bf16[512,768]{1,0:T(8,128)(2,1)S(1)}, u32[]{:S(2)}, u32[]{:S(2)}) %collective-permute-start.12) | collective-permute-done | bytes 786464 | tf_op jit(solution)/shard_map/ppermute | solution.py:249
  272.8 16.9 %collective-permute-done.16.refs_6_ = bf16[512,768]{1,0:T(8,128)(2,1)S(1)} collective-permute-done((bf16[512,768]{1,0:T(8,128)(2,1)S(1)}, bf16[512,768]{1,0:T(8,128)(2,1)S(1)}, u32[]{:S(2)}, u32[]{:S(2)}) %collective-permute-start.16) | collective-permute-done | bytes 786464 | tf_op jit(solution)/shard_map/ppermute | solution.py:249
  289.7 15.2 %collective-permute-done.20.refs_9_ = bf16[512,768]{1,0:T(8,128)(2,1)S(1)} collective-permute-done((bf16[512,768]{1,0:T(8,128)(2,1)S(1)}, bf16[512,768]{1,0:T(8,128)(2,1)S(1)}, u32[]{:S(2)}, u32[]{:S(2)}) %collective-permute-start.20) | collective-permute-done | bytes 786464 | tf_op jit(solution)/shard_map/ppermute | solution.py:249
  304.9 7.9 %product.20.refs_0_ = bf16[1536,768]{1,0:T(8,128)(2,1)} custom-call(s32[1]{0:T(128)} %bitcast.1.slots, bf16[2,1536,768]{2,1,0:T(8,128)(2,1)} %copy-done, bf16[512,1536]{1,0:T(8,128)(2,1)S(1)} %copy-done.3, bf16[512,1536]{1,0:T(8,128)(2,1)S(1)} %constant_dynamic-update-slice_fusion.2.refs_2_, bf16[512,768]{1,0:T(8,128)(2,1)S(1)} %collective-permute-done.12.refs_3_, ...), custom_call_target="tpu_custom_call" | custom-call | flops 3623878656 | bytes 11796480 | tf_op jit(solution)/shard_map/product/pallas_call | solution.py:153
  318.3 8.1 %collective-permute-done.24.refs_3_ = bf16[512,384]{1,0:T(8,128)(2,1)S(1)} collective-permute-done((bf16[512,384]{1,0:T(8,128)(2,1)S(1)}, bf16[512,384]{1,0:T(8,128)(2,1)S(1)}, u32[]{:S(2)}, u32[]{:S(2)}) %collective-permute-start.24) | collective-permute-done | bytes 393248 | tf_op jit(solution)/shard_map/ppermute | solution.py:249
  328.2 6.4 %collective-permute-done.30.refs_3_ = bf16[512,384]{1,0:T(8,128)(2,1)S(1)} collective-permute-done((bf16[512,384]{1,0:T(8,128)(2,1)}, bf16[512,384]{1,0:T(8,128)(2,1)S(1)}, u32[]{:S(2)}, u32[]{:S(2)}) %collective-permute-start.30) | collective-permute-done | bytes 393248 | tf_op jit(solution)/shard_map/ppermute | solution.py:249
  351.4 3.6 collective-permute-done.27
  357.3 6.6 %collective-permute-done.28 = bf16[512,384]{1,0:T(8,128)(2,1)} collective-permute-done((bf16[512,384]{1,0:T(8,128)(2,1)S(1)}, bf16[512,384]{1,0:T(8,128)(2,1)}, u32[]{:S(2)}, u32[]{:S(2)}) %collective-permute-start.28) | collective-permute-done | bytes 393248 | tf_op jit(solution)/shard_map/ppermute | solution.py:246
  365.2 6.6 %collective-permute-done.32 = bf16[512,384]{1,0:T(8,128)(2,1)S(1)} collective-permute-done((bf16[512,384]{1,0:T(8,128)(2,1)S(1)}, bf16[512,384]{1,0:T(8,128)(2,1)S(1)}, u32[]{:S(2)}, u32[]{:S(2)}) %collective-permute-start.32) | collective-permute-done | bytes 393248 | tf_op jit(solution)/shard_map/ppermute | solution.py:246
  372.0 8.5 %collective-permute-done.34 = bf16[512,384]{1,0:T(8,128)(2,1)S(1)} collective-permute-done((bf16[512,384]{1,0:T(8,128)(2,1)S(1)}, bf16[512,384]{1,0:T(8,128)(2,1)S(1)}, u32[]{:S(2)}, u32[]{:S(2)}) %collective-permute-start.34) | collective-permute-done | bytes 393248 | tf_op jit(solution)/shard_map/ppermute | solution.py:246
  (144 shorter events, 84.4 us)
Async XLA Ops:
  1.9 15.8 %collective-permute-start = (bf16[512,512]{1,0:T(8,128)(2,1)S(1)}, bf16[512,512]{1,0:T(8,128)(2,1)S(1)}, u32[]{:S(2)}, u32[]{:S(2)}) collective-permute-start(bf16[512,512]{1,0:T(8,128)(2,1)S(1)} %constant_dynamic-update-slice_fusion), channel_id=1, source_target_pairs={{0,8},{4,12},{8,0},{12,4},{16,24},{20,28},{24,16},{28,20},{1,9},{5... | collective-permute-start | bytes 1572872 | tf_op jit(solution)/shard_map/ppermute | solution.py:246
  4.9 24.6 %collective-permute-start.1 = (bf16[512,512]{1,0:T(8,128)(2,1)S(1)}, bf16[512,512]{1,0:T(8,128)(2,1)S(1)}, u32[]{:S(2)}, u32[]{:S(2)}) collective-permute-start(bf16[512,512]{1,0:T(8,128)(2,1)S(1)} %constant_dynamic-update-slice_fusion), channel_id=1, source_target_pairs={{0,16},{4,20},{8,24},{12,28},{16,0},{20,4},{24,8},{28,12},{1,17},{... | collective-permute-start | bytes 1572872 | tf_op jit(solution)/shard_map/ppermute | solution.py:246
  6.5 23.9 %collective-permute-start.2 = (bf16[512,512]{1,0:T(8,128)(2,1)S(1)}, bf16[512,512]{1,0:T(8,128)(2,1)}, u32[]{:S(2)}, u32[]{:S(2)}) collective-permute-start(bf16[512,512]{1,0:T(8,128)(2,1)S(1)} %constant_dynamic-update-slice_fusion), channel_id=1, source_target_pairs={{0,24},{4,28},{8,16},{12,20},{16,8},{20,12},{24,0},{28,4},{1,25},{... | collective-permute-start | bytes 1572872 | tf_op jit(solution)/shard_map/ppermute | solution.py:246
  33.1 32.5 %collective-permute-start.3 = (bf16[1536,768]{1,0:T(8,128)(2,1)}, bf16[1536,768]{1,0:T(8,128)(2,1)}, u32[]{:S(2)}, u32[]{:S(2)}) collective-permute-start(bf16[1536,768]{1,0:T(8,128)(2,1)} %get-tuple-element.23), channel_id=1, source_target_pairs={{4,16},{12,24},{16,4},{24,12},{5,17},{13,25},{17,5},{25,13},{6,18}... | collective-permute-start | bytes 7077896 | tf_op jit(solution)/shard_map/ppermute | solution.py:269
  36.5 53.6 %collective-permute-start.6 = (bf16[1536,768]{1,0:T(8,128)(2,1)}, bf16[1536,768]{1,0:T(8,128)(2,1)}, u32[]{:S(2)}, u32[]{:S(2)}) collective-permute-start(bf16[1536,768]{1,0:T(8,128)(2,1)} %get-tuple-element.26), channel_id=1, source_target_pairs={{0,8},{4,24},{8,0},{12,16},{16,12},{20,28},{24,4},{28,20},{1,9},{5... | collective-permute-start | bytes 7077896 | tf_op jit(solution)/shard_map/ppermute | solution.py:269
  69.5 24.4 %collective-permute-start.5 = (bf16[1536,768]{1,0:T(8,128)(2,1)}, bf16[1536,768]{1,0:T(8,128)(2,1)}, u32[]{:S(2)}, u32[]{:S(2)}) collective-permute-start(bf16[1536,768]{1,0:T(8,128)(2,1)} %broadcast_select_fusion), channel_id=1, source_target_pairs={{0,4},{4,0},{8,12},{12,8},{16,20},{20,16},{24,28},{28,24},{1,5},{5... | collective-permute-start | bytes 7077896 | tf_op jit(solution)/shard_map/ppermute | solution.py:246
  90.1 13.8 %collective-permute-start.7 = (bf16[1536,768]{1,0:T(8,128)(2,1)}, bf16[1536,768]{1,0:T(8,128)(2,1)}, u32[]{:S(2)}, u32[]{:S(2)}) collective-permute-start(bf16[1536,768]{1,0:T(8,128)(2,1)} %collective-permute-done.6), channel_id=1, source_target_pairs={{0,4},{4,0},{8,12},{12,8},{16,20},{20,16},{24,28},{28,24},{1,5},{5... | collective-permute-start | bytes 7077896 | tf_op jit(solution)/shard_map/ppermute | solution.py:246
  91.3 36.3 %collective-permute-start.13 = (bf16[512,1536]{1,0:T(8,128)(2,1)S(1)}, bf16[512,1536]{1,0:T(8,128)(2,1)S(1)}, u32[]{:S(2)}, u32[]{:S(2)}) collective-permute-start(bf16[512,1536]{1,0:T(8,128)(2,1)S(1)} %attend.1.refs_1_), channel_id=1, source_target_pairs={{0,8},{4,12},{8,0},{12,4},{16,24},{20,28},{24,16},{28,20},{1,9},{5... | collective-permute-start | bytes 4718600 | tf_op jit(solution)/shard_map/ppermute | solution.py:246
  91.8 46.9 %collective-permute-start.17 = (bf16[512,1536]{1,0:T(8,128)(2,1)S(1)}, bf16[512,1536]{1,0:T(8,128)(2,1)S(1)}, u32[]{:S(2)}, u32[]{:S(2)}) collective-permute-start(bf16[512,1536]{1,0:T(8,128)(2,1)S(1)} %attend.1.refs_1_), channel_id=1, source_target_pairs={{0,16},{4,20},{8,24},{12,28},{16,0},{20,4},{24,8},{28,12},{1,17},{... | collective-permute-start | bytes 4718600 | tf_op jit(solution)/shard_map/ppermute | solution.py:246
  100.3 21.4 %collective-permute-start.8 = (bf16[512,768]{1,0:T(8,128)(2,1)S(1)}, bf16[512,768]{1,0:T(8,128)(2,1)S(1)}, u32[]{:S(2)}, u32[]{:S(2)}) collective-permute-start(bf16[512,768]{1,0:T(8,128)(2,1)S(1)} %product.13), channel_id=1, source_target_pairs={{0,1},{3,2},{4,5},{7,6},{8,9},{11,10},{12,13},{15,14},{16,17},{19,... | collective-permute-start | bytes 2359304 | tf_op jit(solution)/shard_map/ppermute | solution.py:249
  110.3 28.3 %collective-permute-start.10 = (bf16[512,768]{1,0:T(8,128)(2,1)S(1)}, bf16[512,768]{1,0:T(8,128)(2,1)S(1)}, u32[]{:S(2)}, u32[]{:S(2)}) collective-permute-start(bf16[512,768]{1,0:T(8,128)(2,1)S(1)} %product.14), channel_id=1, source_target_pairs={{0,1},{3,2},{4,5},{7,6},{8,9},{11,10},{12,13},{15,14},{16,17},{19,... | collective-permute-start | bytes 2359304 | tf_op jit(solution)/shard_map/ppermute | solution.py:249
  121.9 16.8 %collective-permute-start.9 = (bf16[512,768]{1,0:T(8,128)(2,1)S(1)}, bf16[512,768]{1,0:T(8,128)(2,1)S(1)}, u32[]{:S(2)}, u32[]{:S(2)}) collective-permute-start(bf16[512,768]{1,0:T(8,128)(2,1)S(1)} %add_convert_fusion.4), channel_id=1, source_target_pairs={{1,2},{2,1},{5,6},{6,5},{9,10},{10,9},{13,14},{14,13},{17,18},{18,... | collective-permute-start | bytes 2359304 | tf_op jit(solution)/shard_map/ppermute | solution.py:249
  132.8 39.5 %collective-permute-start.14 = (bf16[512,1536]{1,0:T(8,128)(2,1)S(1)}, bf16[512,1536]{1,0:T(8,128)(2,1)S(1)}, u32[]{:S(2)}, u32[]{:S(2)}) collective-permute-start(bf16[512,1536]{1,0:T(8,128)(2,1)S(1)} %product.16), channel_id=1, source_target_pairs={{0,1},{3,2},{4,5},{7,6},{8,9},{11,10},{12,13},{15,14},{16,17},{19,... | collective-permute-start | bytes 4718600 | tf_op jit(solution)/shard_map/ppermute | solution.py:249
  144.9 60.5 %collective-permute-start.18 = (bf16[512,1536]{1,0:T(8,128)(2,1)S(1)}, bf16[512,1536]{1,0:T(8,128)(2,1)S(1)}, u32[]{:S(2)}, u32[]{:S(2)}) collective-permute-start(bf16[512,1536]{1,0:T(8,128)(2,1)S(1)} %product.18), channel_id=1, source_target_pairs={{0,1},{3,2},{4,5},{7,6},{8,9},{11,10},{12,13},{15,14},{16,17},{19,... | collective-permute-start | bytes 4718600 | tf_op jit(solution)/shard_map/ppermute | solution.py:249
  152.8 56.0 %collective-permute-start.21 = (bf16[512,1536]{1,0:T(8,128)(2,1)S(1)}, bf16[512,1536]{1,0:T(8,128)(2,1)S(1)}, u32[]{:S(2)}, u32[]{:S(2)}) collective-permute-start(bf16[512,1536]{1,0:T(8,128)(2,1)S(1)} %attend.1.refs_1_), channel_id=1, source_target_pairs={{0,24},{4,28},{8,16},{12,20},{16,8},{20,12},{24,0},{28,4},{1,25},{... | collective-permute-start | bytes 4718600 | tf_op jit(solution)/shard_map/ppermute | solution.py:246
  154.1 54.7 %collective-permute-start.11 = (bf16[512,768]{1,0:T(8,128)(2,1)S(1)}, bf16[512,768]{1,0:T(8,128)(2,1)S(1)}, u32[]{:S(2)}, u32[]{:S(2)}) collective-permute-start(bf16[512,768]{1,0:T(8,128)(2,1)S(1)} %add_convert_fusion.3), channel_id=1, source_target_pairs={{1,2},{2,1},{5,6},{6,5},{9,10},{10,9},{13,14},{14,13},{17,18},{18,... | collective-permute-start | bytes 2359304 | tf_op jit(solution)/shard_map/ppermute | solution.py:249
  173.8 54.0 %collective-permute-start.15 = (bf16[512,1536]{1,0:T(8,128)(2,1)}, bf16[512,1536]{1,0:T(8,128)(2,1)}, u32[]{:S(2)}, u32[]{:S(2)}) collective-permute-start(bf16[512,1536]{1,0:T(8,128)(2,1)} %add_convert_fusion.2), channel_id=1, source_target_pairs={{1,2},{2,1},{5,6},{6,5},{9,10},{10,9},{13,14},{14,13},{17,18},{18,... | collective-permute-start | bytes 4718600 | tf_op jit(solution)/shard_map/ppermute | solution.py:249
  207.0 26.1 %collective-permute-start.19 = (bf16[512,1536]{1,0:T(8,128)(2,1)}, bf16[512,1536]{1,0:T(8,128)(2,1)}, u32[]{:S(2)}, u32[]{:S(2)}) collective-permute-start(bf16[512,1536]{1,0:T(8,128)(2,1)} %add_convert_fusion.1), channel_id=1, source_target_pairs={{1,2},{2,1},{5,6},{6,5},{9,10},{10,9},{13,14},{14,13},{17,18},{18,... | collective-permute-start | bytes 4718600 | tf_op jit(solution)/shard_map/ppermute | solution.py:249
  214.7 41.4 %collective-permute-start.22 = (bf16[512,1536]{1,0:T(8,128)(2,1)}, bf16[512,1536]{1,0:T(8,128)(2,1)}, u32[]{:S(2)}, u32[]{:S(2)}) collective-permute-start(bf16[512,1536]{1,0:T(8,128)(2,1)} %product.21), channel_id=1, source_target_pairs={{0,1},{3,2},{4,5},{7,6},{8,9},{11,10},{12,13},{15,14},{16,17},{19,... | collective-permute-start | bytes 4718600 | tf_op jit(solution)/shard_map/ppermute | solution.py:249
  227.7 45.1 %collective-permute-start.12 = (bf16[512,768]{1,0:T(8,128)(2,1)S(1)}, bf16[512,768]{1,0:T(8,128)(2,1)S(1)}, u32[]{:S(2)}, u32[]{:S(2)}) collective-permute-start(bf16[512,768]{1,0:T(8,128)(2,1)S(1)} %product.15), channel_id=1, source_target_pairs={{0,1},{1,0},{2,3},{3,2},{4,5},{5,4},{6,7},{7,6},{8,9},{9,8},{10,11... | collective-permute-start | bytes 2359304 | tf_op jit(solution)/shard_map/ppermute | solution.py:249
  231.1 58.5 %collective-permute-start.16 = (bf16[512,768]{1,0:T(8,128)(2,1)S(1)}, bf16[512,768]{1,0:T(8,128)(2,1)S(1)}, u32[]{:S(2)}, u32[]{:S(2)}) collective-permute-start(bf16[512,768]{1,0:T(8,128)(2,1)S(1)} %product.17), channel_id=1, source_target_pairs={{0,1},{1,0},{2,3},{3,2},{4,5},{5,4},{6,7},{7,6},{8,9},{9,8},{10,11... | collective-permute-start | bytes 2359304 | tf_op jit(solution)/shard_map/ppermute | solution.py:249
  236.3 68.6 %collective-permute-start.20 = (bf16[512,768]{1,0:T(8,128)(2,1)S(1)}, bf16[512,768]{1,0:T(8,128)(2,1)S(1)}, u32[]{:S(2)}, u32[]{:S(2)}) collective-permute-start(bf16[512,768]{1,0:T(8,128)(2,1)S(1)} %product.19), channel_id=1, source_target_pairs={{0,1},{1,0},{2,3},{3,2},{4,5},{5,4},{6,7},{7,6},{8,9},{9,8},{10,11... | collective-permute-start | bytes 2359304 | tf_op jit(solution)/shard_map/ppermute | solution.py:249
  259.6 53.1 %collective-permute-start.23 = (bf16[512,1536]{1,0:T(8,128)(2,1)}, bf16[512,1536]{1,0:T(8,128)(2,1)S(1)}, u32[]{:S(2)}, u32[]{:S(2)}) collective-permute-start(bf16[512,1536]{1,0:T(8,128)(2,1)} %add_convert_fusion), channel_id=1, source_target_pairs={{1,2},{2,1},{5,6},{6,5},{9,10},{10,9},{13,14},{14,13},{17,18},{18,... | collective-permute-start | bytes 4718600 | tf_op jit(solution)/shard_map/ppermute | solution.py:249
  312.8 27.3 %collective-permute-start.25 = (bf16[1536,768]{1,0:T(8,128)(2,1)}, bf16[1536,768]{1,0:T(8,128)(2,1)}, u32[]{:S(2)}, u32[]{:S(2)}) collective-permute-start(bf16[1536,768]{1,0:T(8,128)(2,1)} %product.20.refs_0_), channel_id=1, source_target_pairs={{0,4},{4,0},{8,12},{12,8},{16,20},{20,16},{24,28},{28,24},{1,5},{5... | collective-permute-start | bytes 7077896 | tf_op jit(solution)/shard_map/ppermute | solution.py:246
  313.8 12.5 %collective-permute-start.24 = (bf16[512,384]{1,0:T(8,128)(2,1)S(1)}, bf16[512,384]{1,0:T(8,128)(2,1)S(1)}, u32[]{:S(2)}, u32[]{:S(2)}) collective-permute-start(bf16[512,384]{1,0:T(8,128)(2,1)S(1)} %product.22), channel_id=1, source_target_pairs={{0,1},{1,0},{2,3},{3,2},{4,5},{5,4},{6,7},{7,6},{8,9},{9,8},{10,11... | collective-permute-start | bytes 1179656 | tf_op jit(solution)/shard_map/ppermute | solution.py:249
  318.2 16.4 %collective-permute-start.30 = (bf16[512,384]{1,0:T(8,128)(2,1)}, bf16[512,384]{1,0:T(8,128)(2,1)S(1)}, u32[]{:S(2)}, u32[]{:S(2)}) collective-permute-start(bf16[512,384]{1,0:T(8,128)(2,1)} %product.24), channel_id=1, source_target_pairs={{0,1},{1,0},{2,3},{3,2},{4,5},{5,4},{6,7},{7,6},{8,9},{9,8},{10,11... | collective-permute-start | bytes 1179656 | tf_op jit(solution)/shard_map/ppermute | solution.py:249
  342.9 12.1 %collective-permute-start.27 = (bf16[512,384]{1,0:T(8,128)(2,1)S(1)}, bf16[512,384]{1,0:T(8,128)(2,1)}, u32[]{:S(2)}, u32[]{:S(2)}) collective-permute-start(bf16[512,384]{1,0:T(8,128)(2,1)S(1)} %get-tuple-element.34), channel_id=1, source_target_pairs={{0,8},{4,12},{8,0},{12,4},{16,24},{20,28},{24,16},{28,20},{1,9},{5... | collective-permute-start | bytes 1179656 | tf_op jit(solution)/shard_map/ppermute | solution.py:246
  343.5 20.3 %collective-permute-start.28 = (bf16[512,384]{1,0:T(8,128)(2,1)S(1)}, bf16[512,384]{1,0:T(8,128)(2,1)}, u32[]{:S(2)}, u32[]{:S(2)}) collective-permute-start(bf16[512,384]{1,0:T(8,128)(2,1)S(1)} %get-tuple-element.35), channel_id=1, source_target_pairs={{0,16},{4,20},{8,24},{12,28},{16,0},{20,4},{24,8},{28,12},{1,17},{... | collective-permute-start | bytes 1179656 | tf_op jit(solution)/shard_map/ppermute | solution.py:246
  344.7 20.2 %collective-permute-start.29 = (bf16[512,384]{1,0:T(8,128)(2,1)S(1)}, bf16[512,384]{1,0:T(8,128)(2,1)S(1)}, u32[]{:S(2)}, u32[]{:S(2)}) collective-permute-start(bf16[512,384]{1,0:T(8,128)(2,1)S(1)} %get-tuple-element.36), channel_id=1, source_target_pairs={{0,24},{4,28},{8,16},{12,20},{16,8},{20,12},{24,0},{28,4},{1,25},{... | collective-permute-start | bytes 1179656 | tf_op jit(solution)/shard_map/ppermute | solution.py:246
  349.2 22.6 %collective-permute-start.32 = (bf16[512,384]{1,0:T(8,128)(2,1)S(1)}, bf16[512,384]{1,0:T(8,128)(2,1)S(1)}, u32[]{:S(2)}, u32[]{:S(2)}) collective-permute-start(bf16[512,384]{1,0:T(8,128)(2,1)S(1)} %get-tuple-element.38), channel_id=1, source_target_pairs={{0,8},{4,12},{8,0},{12,4},{16,24},{20,28},{24,16},{28,20},{1,9},{5... | collective-permute-start | bytes 1179656 | tf_op jit(solution)/shard_map/ppermute | solution.py:246
  349.8 22.1 %collective-permute-start.33 = (bf16[512,384]{1,0:T(8,128)(2,1)S(1)}, bf16[512,384]{1,0:T(8,128)(2,1)S(1)}, u32[]{:S(2)}, u32[]{:S(2)}) collective-permute-start(bf16[512,384]{1,0:T(8,128)(2,1)S(1)} %get-tuple-element.39), channel_id=1, source_target_pairs={{0,16},{4,20},{8,24},{12,28},{16,0},{20,4},{24,8},{28,12},{1,17},{... | collective-permute-start | bytes 1179656 | tf_op jit(solution)/shard_map/ppermute | solution.py:246
  355.0 25.5 %collective-permute-start.34 = (bf16[512,384]{1,0:T(8,128)(2,1)S(1)}, bf16[512,384]{1,0:T(8,128)(2,1)S(1)}, u32[]{:S(2)}, u32[]{:S(2)}) collective-permute-start(bf16[512,384]{1,0:T(8,128)(2,1)S(1)} %get-tuple-element.40), channel_id=1, source_target_pairs={{0,24},{4,28},{8,16},{12,20},{16,8},{20,12},{24,0},{28,4},{1,25},{... | collective-permute-start | bytes 1179656 | tf_op jit(solution)/shard_map/ppermute | solution.py:246
  (27 other events, 536.1 us)

commit v2 on v1

v2 whole, which is shorter than its diff:
```python
import functools
import math
import jax
import jax.numpy as jnp
from jax import lax
from jax.experimental import pallas as pl
from jax.experimental.pallas import tpu as pltpu
from jax.sharding import PartitionSpec as P
HEAD_DIM = 128
WINDOW = 4096
BLOCK = 128
KEY_TILE = 512
MASKED = -1e+30
SCALE = math.log2(math.e) / math.sqrt(HEAD_DIM)

def attention_kernel(group, kv_heads, n_kv, place, low, high, rows_at, q_ref, qseg_ref, seg_ref, *refs):
    kv_refs, (out_ref, packed_kv, score_ref, top_ref, total_ref, acc_ref) = (refs[:n_kv], refs[n_kv:])
    step = pl.program_id(0)
    kv_rows = kv_refs[0].shape[0]

    @pl.when(step == 0)
    def _():

        def move(block, _):
            row = rows_at[block]
            for i, kv_ref in enumerate(kv_refs):

                @pl.when((row >= i * kv_rows) & (row < (i + 1) * kv_rows))
                def _(i=i, kv_ref=kv_ref):
                    at = pl.multiple_of(row - i * kv_rows, BLOCK)
                    packed_kv[pl.ds(pl.multiple_of(block * BLOCK, BLOCK), BLOCK), :] = kv_ref[pl.ds(at, BLOCK), :]
            return 0
        lax.fori_loop(0, rows_at.shape[0], move, 0)
    first = place[step] * BLOCK
    q_pos = first + lax.broadcasted_iota(jnp.int32, (BLOCK, KEY_TILE), 0)
    q_seg = qseg_ref[...]
    lo_tile = low[step] // KEY_TILE
    hi_tile = (first + BLOCK - 1) // KEY_TILE + 1
    inner_lo = jnp.minimum((high[step] + KEY_TILE - 1) // KEY_TILE, hi_tile - 1)
    inner_hi = jnp.maximum((first + 1) // KEY_TILE, inner_lo)
    kv_cols = kv_heads * HEAD_DIM
    rows = group * BLOCK
    lanes = [slice(i * HEAD_DIM, (i + 1) * HEAD_DIM) for i in range(KEY_TILE // HEAD_DIM)]
    for kv_head in range(kv_heads):
        q = jnp.concatenate([q_ref[:, (kv_head * group + h) * HEAD_DIM:(kv_head * group + h + 1) * HEAD_DIM] for h in range(group)], axis=0)
        q = (q.astype(jnp.float32) * SCALE).astype(jnp.bfloat16)
        top_ref[...] = jnp.full((rows, HEAD_DIM), MASKED, jnp.float32)

        def score(t, _, masked, q=q, kv_head=kv_head):
            at = pl.ds(pl.multiple_of(t * KEY_TILE, KEY_TILE), KEY_TILE)
            keys = packed_kv[at, kv_head * HEAD_DIM:(kv_head + 1) * HEAD_DIM]
            scores = lax.dot_general(q, keys, (((1,), (1,)), ((), ())), preferred_element_type=jnp.float32)
            if masked:
                k_pos = t * KEY_TILE + lax.broadcasted_iota(jnp.int32, (BLOCK, KEY_TILE), 1)
                kept = (k_pos <= q_pos) & (k_pos > q_pos - WINDOW) & (seg_ref[:, at] == q_seg)
                scores = jnp.where(kept[None], scores.reshape(group, BLOCK, KEY_TILE), MASKED)
                scores = scores.reshape(rows, KEY_TILE)
            score_ref[t - lo_tile] = scores
            most = scores[:, lanes[0]]
            for lane in lanes[1:]:
                most = jnp.maximum(most, scores[:, lane])
            top_ref[...] = jnp.maximum(top_ref[...], most)
            return 0
        lax.fori_loop(lo_tile, inner_lo, functools.partial(score, masked=True), 0)
        lax.fori_loop(inner_lo, inner_hi, functools.partial(score, masked=False), 0)
        lax.fori_loop(inner_hi, hi_tile, functools.partial(score, masked=True), 0)
        top_ref[...] = jnp.broadcast_to(jnp.max(top_ref[...], axis=1, keepdims=True), (rows, HEAD_DIM))
        total_ref[...] = jnp.zeros((rows, HEAD_DIM), jnp.float32)
        acc_ref[...] = jnp.zeros((rows, HEAD_DIM), jnp.float32)

        def weigh(t, _, kv_head=kv_head):
            at = pl.ds(pl.multiple_of(t * KEY_TILE, KEY_TILE), KEY_TILE)
            values = packed_kv[at, kv_cols + kv_head * HEAD_DIM:kv_cols + (kv_head + 1) * HEAD_DIM]
            top = top_ref[...]
            total, parts = (total_ref[...], [])
            for lane in lanes:
                part = jnp.exp2(score_ref[t - lo_tile, :, lane] - top)
                total = total + part
                parts.append(part.astype(jnp.bfloat16))
            total_ref[...] = total
            expo = jnp.concatenate(parts, axis=1)
            acc_ref[...] += jnp.dot(expo, values, preferred_element_type=jnp.float32)
            return 0
        lax.fori_loop(lo_tile, hi_tile, weigh, 0)
        heads = (acc_ref[...] / jnp.sum(total_ref[...], axis=1, keepdims=True)).astype(jnp.bfloat16)
        for h in range(group):
            to = (kv_head * group + h) * HEAD_DIM
            out_ref[:, to:to + HEAD_DIM] = heads[h * BLOCK:(h + 1) * BLOCK]

def attend(q, kv, rows_at, place, segment_ids, first=0):
    blocks = place.shape[0]
    tokens = segment_ids.shape[0]
    kv_heads = kv[0].shape[1] // (2 * HEAD_DIM)
    group = q.shape[1] // HEAD_DIM // kv_heads
    q_seg = segment_ids.reshape(-1, BLOCK)[place]
    doc_first = jnp.sum((segment_ids[None, :] < q_seg[:, :1]).astype(jnp.int32), axis=1)
    low = jnp.maximum(doc_first, place * BLOCK - (WINDOW - 1))
    last_first = jnp.sum((segment_ids[None, :] < q_seg[:, -1:]).astype(jnp.int32), axis=1)
    high = jnp.maximum(last_first, place * BLOCK + BLOCK - WINDOW)
    tiles = min(tokens // KEY_TILE, WINDOW // KEY_TILE + 2)
    rows = group * BLOCK
    grid = pltpu.PrefetchScalarGridSpec(num_scalar_prefetch=4, grid=(blocks,), in_specs=[pl.BlockSpec((BLOCK, q.shape[1]), lambda i, *_: (first + i, 0)), pl.BlockSpec((BLOCK, 1), lambda i, *_: (i, 0)), pl.BlockSpec((1, tokens), lambda i, *_: (0, 0))] + [pl.BlockSpec(part.shape, lambda i, *_: (0, 0)) for part in kv], out_specs=pl.BlockSpec((BLOCK, q.shape[1]), lambda i, *_: (i, 0)), scratch_shapes=[pltpu.VMEM((tokens, kv[0].shape[1]), jnp.bfloat16), pltpu.VMEM((tiles, rows, KEY_TILE), jnp.float32)] + [pltpu.VMEM((rows, HEAD_DIM), jnp.float32)] * 3)
    rows = blocks * BLOCK
    return pl.pallas_call(functools.partial(attention_kernel, group, kv_heads, len(kv)), grid_spec=grid, out_shape=jax.ShapeDtypeStruct((rows, q.shape[1]), jnp.bfloat16), compiler_params=pltpu.CompilerParams(vmem_limit_bytes=48 << 20), cost_estimate=pl.CostEstimate(flops=4 * rows * q.shape[1] * tokens // 2, bytes_accessed=4 * rows * q.shape[1] + 2 * tokens * kv[0].shape[1], transcendentals=rows * (q.shape[1] // HEAD_DIM) * tokens // 2), name='attend')(place, low, high, rows_at, q, q_seg.reshape(-1, 1), segment_ids.reshape(1, -1), *kv)

def product_kernel(layout, kinds, slots, *refs):
    out_ref = refs[-1]

    def write(w_ref):
        row = 0
        for h, adds in layout:
            total = jnp.dot(refs[h][...], w_ref[...], preferred_element_type=jnp.float32)
            for a in adds:
                total = total + refs[a][...].astype(jnp.float32)
            rows = total.shape[0]
            out_ref[row:row + rows, :] = total.astype(out_ref.dtype)
            row += rows
    if kinds == 1:
        write(refs[0])
    else:
        for k in range(kinds):
            pl.when(slots[0] == k)(functools.partial(write, refs[k]))

def product(parts, weight, slots, adds=None, tile=384, first=0, tiles=None):
    kinds = len(weight) if isinstance(weight, list) else 1
    depth, cols = (weight[0] if kinds > 1 else weight).shape[-2:]
    per_group = cols // tile
    tiles = tiles or per_group
    if kinds > 1:
        operands = list(weight)
        in_specs = [pl.BlockSpec((depth, tile), lambda g, j, s, k=k: (0, jnp.where(s[0] == k, first + j, first))) for k in range(kinds)]
    else:
        operands = [weight]
        in_specs = [pl.BlockSpec((None, depth, tile), lambda g, j, s: (s[g], 0, first + j))]
    layout = []
    for p, h in enumerate(parts):
        rows = h.shape[0]
        operands.append(h)
        in_specs.append(pl.BlockSpec((rows, depth), lambda g, j, s: (0, 0)))
        at, more = (len(operands) - 1, [])
        for a, r, slotted in adds[p] if adds else ():
            operands.append(a)
            if slotted:
                in_specs.append(pl.BlockSpec((rows, tile), lambda g, j, s, r=r: (r, s[g] * per_group + first + j)))
            else:
                in_specs.append(pl.BlockSpec((rows, tile), lambda g, j, s, r=r: (r, g * tiles + j)))
            more.append(len(operands) - 1)
        layout.append((at, more))
    rows = sum((h.shape[0] for h in parts))
    groups = slots.shape[0]
    return pl.pallas_call(functools.partial(product_kernel, layout, kinds), grid_spec=pltpu.PrefetchScalarGridSpec(num_scalar_prefetch=1, grid=(groups, tiles), in_specs=in_specs, out_specs=pl.BlockSpec((rows, tile), lambda g, j, s: (0, g * tiles + j))), out_shape=jax.ShapeDtypeStruct((rows, groups * tiles * tile), jnp.bfloat16), compiler_params=pltpu.CompilerParams(vmem_limit_bytes=40 << 20), cost_estimate=pl.CostEstimate(flops=int(1 * 2 * rows * depth * groups * tiles * tile), bytes_accessed=int(1 * (2 * depth * (rows + groups * tiles * tile) + 4 * rows * groups * tiles * tile)), transcendentals=0), name='product')(slots, *operands)

def pick_kernel(pools, source, *refs):
    outs = refs[pools:]
    per_out = outs[0].shape[0] // BLOCK
    for i in range(source.shape[0]):
        row = source[i] * BLOCK
        out = outs[i // per_out]
        to = slice(i % per_out * BLOCK, (i % per_out + 1) * BLOCK)
        low = 0
        for pool in refs[:pools]:

            @pl.when((row >= low) & (row < low + pool.shape[0]))
            def _(pool=pool, row=row, out=out, to=to, low=low):
                out[to, :] = pool[pl.ds(pl.multiple_of(row - low, BLOCK), BLOCK), :]
            low += pool.shape[0]

def pick_blocks(pools, cols, source, outs):
    rows = source.shape[0] * BLOCK // outs
    size = 2 * cols * (sum((p.shape[0] for p, _ in pools)) + rows * outs)
    return pl.pallas_call(functools.partial(pick_kernel, len(pools)), grid_spec=pltpu.PrefetchScalarGridSpec(num_scalar_prefetch=1, grid=(1,), in_specs=[pl.BlockSpec((p.shape[0], cols), lambda i, s, g=g: (0, g)) for p, g in pools], out_specs=[pl.BlockSpec((rows, cols), lambda i, s: (0, 0))] * outs), out_shape=[jax.ShapeDtypeStruct((rows, cols), jnp.bfloat16)] * outs, compiler_params=pltpu.CompilerParams(vmem_limit_bytes=40 << 20), cost_estimate=pl.CostEstimate(flops=0, bytes_accessed=size, transcendentals=0), name='pick_blocks')(source, *[p for p, _ in pools])

def sources_of(packing, per_shard):
    blocks = packing.shape[0]
    target = packing[:, 0] * per_shard + packing[:, 1]
    at = jnp.arange(blocks, dtype=jnp.int32)
    return (target, jnp.sum(jnp.where(target[None, :] == at[:, None], at[None, :], 0), axis=1))

def plain_plan(queries, keys, values, segment_ids, packing, out_weight):
    tok_rows = queries.shape[0]
    per_shard = tok_rows // BLOCK
    me = lax.axis_index('seq')
    target, source = sources_of(packing, per_shard)
    place = lax.dynamic_slice_in_dim(target, me * per_shard, per_shard, 0)
    kv = lax.all_gather(jnp.concatenate([keys, values], axis=1), 'seq', axis=0, tiled=True)
    heads = attend(queries, [kv], source * BLOCK, place, segment_ids)
    heads = lax.all_gather(heads, 'seq', axis=0, tiled=True)
    own = lax.dynamic_slice_in_dim(source, me * per_shard, per_shard, 0)
    heads = heads.reshape(-1, BLOCK, heads.shape[1])[own].reshape(tok_rows, -1)
    weight = lax.all_gather(out_weight, 'seq', axis=1, tiled=True)
    terms = jnp.dot(heads, weight, preferred_element_type=jnp.float32).astype(jnp.bfloat16)
    return lax.psum_scatter(terms, 'tp', scatter_dimension=1, tiled=True)

def after(array, *others):
    return lax.optimization_barrier((array, *others))[0]

def paired_plan(queries, keys, values, segment_ids, packing, out_weight):
    tok_rows, q_cols = queries.shape
    per_shard = tok_rows // BLOCK
    quarter = out_weight.shape[1] // 2
    half = quarter // 2
    me, z = (lax.axis_index('seq'), lax.axis_index('tp'))
    chip, core = (me // 2, me % 2)
    x, pair = (chip % 2, z // 2)
    target, source = sources_of(packing, per_shard)
    place = lax.dynamic_slice_in_dim(target, me * per_shard, per_shard, 0)

    def across(array, mask):
        return lax.ppermute(array, 'seq', [(i, i ^ mask) for i in range(8)])

    def along(array, *route):
        return lax.ppermute(array, 'tp', route)
    kv = jnp.concatenate([keys, values], axis=1)
    kv_x, kv_y, kv_d = (across(kv, 2), across(kv, 4), across(kv, 6))
    pieces = [lax.dynamic_slice_in_dim(out_weight, (x ^ flip) * quarter, quarter, 1) for flip in range(2)]
    kv_own = jnp.concatenate([kv, after(kv_x, *pieces), kv_y, kv_d], axis=0)
    kv_other = across(kv_own, 1)

    def row_of(block):
        relative = block // per_shard ^ me
        return ((relative >> 1) + 4 * (relative & 1)) * tok_rows + block % per_shard * BLOCK
    weights = []
    for flip, piece in enumerate(pieces):
        route = []
        for s in range(8):
            sy, sx, sa = (s // 4, s // 2 % 2, s % 2)
            d = 4 * sa + 2 * (sx ^ flip) + sy
            if s != d:
                route.append((s, d))
        weights.append(lax.ppermute(after(piece, kv_x, kv_y, kv_d), 'seq', route))
    stays = core == chip // 2
    twins = [(i, i ^ 1) for i in range(8) if i % 2 == i // 4]
    given = lax.ppermute(after(pieces[0], kv_other), 'seq', twins)
    heads = attend(queries, [kv_own, kv_other], row_of(source), place, segment_ids)
    mine = [heads, across(heads, 2), across(heads, 4)]
    here = core == pair
    flips = jnp.arange(2, dtype=jnp.int32)
    returned = lax.ppermute(after(weights[0], heads), 'seq', [(d, s) for s, d in twins])
    crossed = across(after(weights[1], heads), 1)
    kinds = [[pieces[0], weights[0], given, returned], [weights[1], crossed]]
    kind = [jnp.where(here, jnp.where(stays, 3, 2), jnp.where(stays, 0, 1)), here.astype(jnp.int32)]

    def settle(*others):
        own = [jnp.where(stays, pieces[0], after(weights[0], *others)), after(weights[1], *others)]
        other = [jnp.where(stays, after(returned, *others), given), after(crossed, *others)]
        far = jnp.stack([jnp.where(here, o, w) for w, o in zip(own, other)])
        return (far, (own, other))

    def add(a, b):
        return (a.astype(jnp.float32) + b.astype(jnp.float32)).astype(jnp.bfloat16)
    chunks = [(0, 0), (0, 1), (1, None), (2, None), (3, None)]
    last = len(chunks) - 1
    shares, inward = ([], [])
    sums, arrived = ([None] * len(chunks), [None] * len(chunks))

    def pass_on(i, *later):
        sums[i] = add(after(shares[i], *later) if later else shares[i], inward[i])
        arrived[i] = along(sums[i], (1, 2), (2, 1))
    both = None
    for i, (r, flip) in enumerate(chunks):
        if i == 2:
            mine.append(across(after(heads, shares[1], mine[1], mine[2]), 6))
            both, sides = settle(shares[1])
        rows = mine[r]
        if i == 1:
            rows = after(rows, shares[0])
        elif i:
            needs = [s for s in sums[:i - 1] if s is not None]
            needs += [a for a in arrived[:i - 2] if a is not None]
            rows = after(rows, shares[i - 1], *needs, *(mine[1:3] if i == 2 else ()))
        if i < 2:
            share = product([rows], kinds[i], kind[i][None])
        else:
            share = product([rows], both, flips if flip is None else flips[flip:flip + 1])
        shares.append(share)
        inward.append(along(share, (0, 1), (3, 2)))
        for j in range(i + 1):
            if sums[j] is None and j + (0, 0, 0, 1, 0, 0)[j] <= i and (j < last):
                pass_on(j, *([shares[i]] if i > j else []))
    own, other = sides
    near = jnp.stack([jnp.where(here, after(w, shares[-1]), o) for w, o in zip(own, other)])
    own_slot = (z & 1 ^ x).astype(jnp.int32)[None]
    came = [None] * 4

    def swap(r, first=0, tiles=2):
        share = product([mine[r]], near, 1 - own_slot, [[(came[r], 0, True)]], half, first, tiles)
        return (share, along(share, (0, 1), (1, 0), (2, 3), (3, 2)))

    def total(parts, swapped, first=0, tiles=2):
        adds = [[(came[r], 0, True), (some, 0, False)] for r, some in zip(parts, swapped)]
        return product([mine[r] for r in parts], near, own_slot, adds, half, first, tiles)
    for j in range(last):
        if sums[j] is None:
            pass_on(j, shares[-1])
    came[0] = jnp.concatenate(arrived[:2], axis=1)
    came[1], came[2] = (arrived[2], arrived[3])
    came[3] = None
    swapped, order_of = ({}, ((0, None), (1, None), (2, None), (3, 0), (3, 1)))
    share = None
    for r, h in order_of:
        tiles = 2 if h is None else 1
        if r == 3 and came[3] is None:
            pass_on(last)
            came[3] = arrived[4]
        share, some = swap(r, h or 0, tiles)
        swapped[r, h] = (share, some)
    split = (0, 0) in swapped
    late = [swapped[3, h][1] for h in range(2)]
    if split:
        early = [[swapped[r, h][1] for r in range(3)] for h in range(2)]
        done = [total((0, 1, 2), early[h], h, 1) for h in range(2)]
        done = [(d, across(d, 1)) for d in done]
    else:
        early = [swapped[r, None][1] for r in range(3)]
        done = total((0, 1, 2), early)
        done = [done, across(done, 1)]
    picks = []
    for r in range(4):
        blocks = lax.dynamic_slice_in_dim(source, (me ^ 2 * r) * per_shard, per_shard, 0)
        picks.append(row_of(blocks) // BLOCK)
    picks = jnp.concatenate(picks)
    result = jnp.zeros((tok_rows, 4 * quarter), jnp.bfloat16)
    for h in range(2):
        some = total((3,), [late[h]], h, 1)
        pools = [(d, 0) for d in done[h]] if split else [(d, h) for d in done]
        rows = pick_blocks([pools[0], (some, 0), pools[1], (across(some, 1), 0)], half, picks, 4)
        for r in range(4):
            some = across(rows[r], 2 * r) if r else rows[r]
            result = lax.dynamic_update_slice_in_dim(result, some, (chip ^ r) * quarter + h * half, 1)
    return result

def solution(mesh):
    in_specs = (P('seq', 'tp'), P('seq', 'tp'), P('seq', 'tp'), P(), P(), P('tp', 'seq'))
    out_specs = P('seq', 'tp')
    paired = mesh.shape['seq'] == 8 and mesh.shape['tp'] == 4
    shards = paired_plan if paired else plain_plan
    return jax.shard_map(shards, mesh=mesh, in_specs=in_specs, out_specs=out_specs, check_vma=False)
```

time: 382 us -> 368 us (0.963)
  waiting for transfers between devices: 173 us -> 160 us
  starting transfers between devices: 87 us -> 77.7 us
  local copies, waits for them, and re-layouts: 21.7 us -> 26.9 us
    ppermute x15, waiting for transfers between devices: 123 us -> 86.6 us  [along(): return lax.ppermute(array, 'tp', route)]
    ppermute x18 -> x17, starting transfers between devices: 35.3 us -> 13.5 us  [across(): return lax.ppermute(array, 'seq', [(i, i ^ mask) for i in range(8)])]
    ppermute x2, waiting for transfers between devices: 0.68 us -> 19.5 us  [paired_plan(): weights.append(lax.ppermute(after(piece, kv_x, kv_y, kv_d), 'seq', route))]
    another operation x1 -> x5, other arithmetic: 2.93 us -> 14.8 us  [the longest x2 8.18 us: paired_plan(): jnp.stack([jnp.where(here, after(w, shares[-1]), o) for w, o in zip(own,...]
    broadcast_in_dim x2 -> x0, other arithmetic: 8.16 us -> none  [paired_plan(): far = [jnp.where(here, other, own)[None] for own, other in weights]]
    ppermute x15, starting transfers between devices: 49 us -> 55.3 us  [along(): return lax.ppermute(array, 'tp', route)]
    ppermute x0 -> x2, starting transfers between devices: none -> 6.23 us  [the longest x1 4.93 us: paired_plan(): given = lax.ppermute(after(pieces[0], kv_other), 'seq', twins)]
    unnamed x50 -> x60, local copies, waits for them, and re-layouts: 11.3 us -> 15.2 us
  transfers between devices with their start and end apart: 35 -> 36, of which waited for: 19 -> 17; matrix products, arithmetic and copies ran while one was open for 8% -> 10% of each run, Pallas kernels for 20% -> 21%
where the time goes in v2:
time: 368 us; the launch traced here: 367 us
  waiting for transfers between devices  160 us (43%)
  starting transfers between devices  77.7 us (21%)
  Pallas kernels  75.7 us (21%)
  local copies, waits for them, and re-layouts  26.9 us (7%)
  other arithmetic  26.9 us (7%)
    ppermute x15, waiting for transfers between devices, along(): return lax.ppermute(array, 'tp', route)  86.6 us
    ppermute x15, starting transfers between devices, along(): return lax.ppermute(array, 'tp', route)  55.3 us
    ppermute x17, waiting for transfers between devices, across(): return lax.ppermute(array, 'seq', [(i, i ^ mask) for i in range(8)])  52.5 us
    pallas_call x13, Pallas kernels, product(): pl.pallas_call(functools.partial(product_kernel, layout, kinds), grid_spe...  47.3 us
    pallas_call x1, Pallas kernels, attend(): pl.pallas_call(functools.partial(attention_kernel, group, kv_heads, len(k...  22.9 us
    ppermute x2, waiting for transfers between devices, paired_plan(): weights.append(lax.ppermute(after(piece, kv_x, kv_y, kv_d), 'seq', route))  19.5 us
    unnamed x60, local copies, waits for them, and re-layouts  15.2 us
    ppermute x17, starting transfers between devices, across(): return lax.ppermute(array, 'seq', [(i, i ^ mask) for i in range(8)])  13.5 us
  transfers between devices with their start and end apart: 36, of which 17 were waited for; matrix products, arithmetic and copies ran while one was open for 10% of the time, Pallas kernels for 21%

profile of v2, /device:TPU:0, one launch (start us, length us, event | category | flops | bytes accessed | tf_op | source)
XLA Modules:
  0.0 367.3 jit_solution(3882850063567741074)
XLA Ops:
  6.5 4.9 %constant_dynamic-slice_fusion.2 = (bf16[1536,768]{1,0:T(8,128)(2,1)}, bf16[1536,768]{1,0:T(8,128)(2,1)}) fusion(bf16[1536,1536]{1,0:T(8,128)(2,1)} %param.11, s32[]{:T(128)S(6)} %select_n.191, s32[]{:T(128)S(6)} %select_n.192), kind=kLoop, calls=%fused_computation.35 | loop fusion | bytes 9437192 | tf_op jit(solution)/shard_map/dynamic_slice | solution.py:215
  11.3 6.4 %collective-permute-done = bf16[512,512]{1,0:T(8,128)(2,1)S(1)} collective-permute-done((bf16[512,512]{1,0:T(8,128)(2,1)S(1)}, bf16[512,512]{1,0:T(8,128)(2,1)S(1)}, u32[]{:S(2)}, u32[]{:S(2)}) %collective-permute-start) | collective-permute-done | bytes 524320 | tf_op jit(solution)/shard_map/ppermute | solution.py:209
  17.7 11.9 %collective-permute-done.1 = bf16[512,512]{1,0:T(8,128)(2,1)S(1)} collective-permute-done((bf16[512,512]{1,0:T(8,128)(2,1)S(1)}, bf16[512,512]{1,0:T(8,128)(2,1)S(1)}, u32[]{:S(2)}, u32[]{:S(2)}) %collective-permute-start.1) | collective-permute-done | bytes 524320 | tf_op jit(solution)/shard_map/ppermute | solution.py:209
  37.2 4.9 %collective-permute-start.7 = (bf16[1536,768]{1,0:T(8,128)(2,1)}, bf16[1536,768]{1,0:T(8,128)(2,1)}, u32[]{:S(2)}, u32[]{:S(2)}) collective-permute-start(bf16[1536,768]{1,0:T(8,128)(2,1)} %get-tuple-element.35.refs_0_), channel_id=1, source_target_pairs={{0,4},{8,12},{20,16},{28,24},{1,5},{9,13},{21,17},{29,25},{2,6},{1... | collective-permute-start | bytes 7077896 | tf_op jit(solution)/shard_map/ppermute | solution.py:233
  45.2 22.9 %attend.1.refs_4_.refs_2_.refs_1_ = bf16[512,1536]{1,0:T(8,128)(2,1)S(1)} custom-call(s32[4]{0:T(128)S(1)} %get-tuple-element.64.place, s32[4]{0:T(128)S(1)} %get-tuple-element.68.low, s32[4]{0:T(128)S(1)} %get-tuple-element.67.high, s32[32]{0:T(128)S(1)} %fusion.9.rows_at, bf16[512,1536]{1,0:T(8,128)(2,1)S(1)} %copy-done.21, s32[512,1]{1,0:T(8,128)S(1)} %copy.8.qseg_ref, ...), custom_call_target="tpu_custom_call" | custom-call | flops 6442450944 | bytes 7340032 | tf_op jit(solution)/shard_map/attend/pallas_call | solution.py:104
  69.4 19.5 %collective-permute-done.4.refs_0_ = bf16[1536,768]{1,0:T(8,128)(2,1)} collective-permute-done((bf16[1536,768]{1,0:T(8,128)(2,1)}, bf16[1536,768]{1,0:T(8,128)(2,1)}, u32[]{:S(2)}, u32[]{:S(2)}) %collective-permute-start.4) | collective-permute-done | bytes 2359328 | tf_op jit(solution)/shard_map/ppermute | solution.py:230
  93.1 4.5 %product.13 = bf16[512,768]{1,0:T(8,128)(2,1)S(1)} custom-call(s32[1]{0:T(128)} %bitcast.7.slots, bf16[1536,768]{1,0:T(8,128)(2,1)} %get-tuple-element.35.refs_0_, bf16[1536,768]{1,0:T(8,128)(2,1)} %collective-permute-done.3.refs_1_, bf16[1536,768]{1,0:T(8,128)(2,1)} %collective-permute-done.7.refs_2_, bf16[1536,768]{1,0:T(8,128)(2,1)} %collective-permute-done.8.refs_3_, ...), custom_call_target="tpu_custom_call" | custom-call | flops 1207959552 | bytes 5505024 | tf_op jit(solution)/shard_map/product/pallas_call | solution.py:151
  97.6 3.5 collective-permute-start.12
  101.2 3.8 %product.14 = bf16[512,768]{1,0:T(8,128)(2,1)S(1)} custom-call(s32[1]{0:T(128)} %bitcast.2.slots, bf16[1536,768]{1,0:T(8,128)(2,1)} %collective-permute-done.4.refs_0_, bf16[1536,768]{1,0:T(8,128)(2,1)} %collective-permute-done.6.refs_1_, bf16[512,1536]{1,0:T(8,128)(2,1)S(1)} %attend.1.refs_4_.refs_2_.refs_1_), custom_call_target="tpu_custom_call" | custom-call | flops 1207959552 | bytes 5505024 | tf_op jit(solution)/shard_map/product/pallas_call | solution.py:151
  106.3 4.3 %select_bitcast_fusion.3 = (bf16[1,1536,768]{2,1,0:T(8,128)(2,1)S(1)}, bf16[1536,768]{1,0:T(8,128)(2,1)}) fusion(pred[]{:T(512)S(6)} %eq.32, bf16[1536,768]{1,0:T(8,128)(2,1)} %collective-permute-done.8.refs_3_, bf16[1536,768]{1,0:T(8,128)(2,1)} %collective-permute-done.7.refs_2_, pred[]{:T(512)S(6)} %eq.33, bf16[1536,768]{1,0:T(8,128)(2,1)} %get-tuple-element.35.refs_0_, ...), kind=kLoop, calls=%fused_computation.9 | loop fusion | flops 3538944 | bytes 14155778 | tf_op jit(solution)/shard_map/stack | solution.py:246
  112.9 6.1 %collective-permute-done.12 = bf16[512,768]{1,0:T(8,128)(2,1)S(1)} collective-permute-done((bf16[512,768]{1,0:T(8,128)(2,1)S(1)}, bf16[512,768]{1,0:T(8,128)(2,1)S(1)}, u32[]{:S(2)}, u32[]{:S(2)}) %collective-permute-start.12) | collective-permute-done | bytes 786464 | tf_op jit(solution)/shard_map/ppermute | solution.py:212
  119.9 6.7 %collective-permute-done.10.refs_1_.refs_7_ = bf16[512,1536]{1,0:T(8,128)(2,1)S(1)} collective-permute-done((bf16[512,1536]{1,0:T(8,128)(2,1)S(1)}, bf16[512,1536]{1,0:T(8,128)(2,1)S(1)}, u32[]{:S(2)}, u32[]{:S(2)}) %collective-permute-start.10) | collective-permute-done | bytes 1572896 | tf_op jit(solution)/shard_map/ppermute | solution.py:209
  128.1 5.9 %product.15 = bf16[512,1536]{1,0:T(8,128)(2,1)} custom-call(s32[2]{0:T(128)S(1)} %iota.16.slots, bf16[2,1536,768]{2,1,0:T(8,128)(2,1)S(1)} %pad_maximum_fusion.refs_0_, bf16[512,1536]{1,0:T(8,128)(2,1)S(1)} %collective-permute-done.9.refs_1_.refs_4_), custom_call_target="tpu_custom_call" | custom-call | flops 2415919104 | bytes 9437184 | tf_op jit(solution)/shard_map/product/pallas_call | solution.py:151
  133.9 4.6 %collective-permute-start.15 = (bf16[512,1536]{1,0:T(8,128)(2,1)}, bf16[512,1536]{1,0:T(8,128)(2,1)}, u32[]{:S(2)}, u32[]{:S(2)}) collective-permute-start(bf16[512,1536]{1,0:T(8,128)(2,1)} %product.15), channel_id=1, source_target_pairs={{0,1},{3,2},{4,5},{7,6},{8,9},{11,10},{12,13},{15,14},{16,17},{19,... | collective-permute-start | bytes 4718600 | tf_op jit(solution)/shard_map/ppermute | solution.py:212
  141.5 5.9 %product.16 = bf16[512,1536]{1,0:T(8,128)(2,1)} custom-call(s32[2]{0:T(128)S(1)} %iota.15.slots, bf16[2,1536,768]{2,1,0:T(8,128)(2,1)S(1)} %pad_maximum_fusion.refs_0_, bf16[512,1536]{1,0:T(8,128)(2,1)S(1)} %collective-permute-done.10.refs_1_.refs_7_), custom_call_target="tpu_custom_call" | custom-call | flops 2415919104 | bytes 9437184 | tf_op jit(solution)/shard_map/product/pallas_call | solution.py:151
  147.4 3.9 %collective-permute-start.20 = (bf16[512,1536]{1,0:T(8,128)(2,1)}, bf16[512,1536]{1,0:T(8,128)(2,1)}, u32[]{:S(2)}, u32[]{:S(2)}) collective-permute-start(bf16[512,1536]{1,0:T(8,128)(2,1)} %product.16), channel_id=1, source_target_pairs={{0,1},{3,2},{4,5},{7,6},{8,9},{11,10},{12,13},{15,14},{16,17},{19,... | collective-permute-start | bytes 4718600 | tf_op jit(solution)/shard_map/ppermute | solution.py:212
  153.7 18.8 %collective-permute-done.15 = bf16[512,1536]{1,0:T(8,128)(2,1)} collective-permute-done((bf16[512,1536]{1,0:T(8,128)(2,1)}, bf16[512,1536]{1,0:T(8,128)(2,1)}, u32[]{:S(2)}, u32[]{:S(2)}) %collective-permute-start.15) | collective-permute-done | bytes 1572896 | tf_op jit(solution)/shard_map/ppermute | solution.py:212
  176.0 5.2 %product.17 = bf16[512,1536]{1,0:T(8,128)(2,1)S(1)} custom-call(s32[2]{0:T(128)S(1)} %iota.14.slots, bf16[2,1536,768]{2,1,0:T(8,128)(2,1)S(1)} %copy-done.13, bf16[512,1536]{1,0:T(8,128)(2,1)S(1)} %collective-permute-done.11.refs_1_), custom_call_target="tpu_custom_call" | custom-call | flops 2415919104 | bytes 9437184 | tf_op jit(solution)/shard_map/product/pallas_call | solution.py:151
  181.1 5.5 %collective-permute-start.23 = (bf16[512,1536]{1,0:T(8,128)(2,1)S(1)}, bf16[512,1536]{1,0:T(8,128)(2,1)}, u32[]{:S(2)}, u32[]{:S(2)}) collective-permute-start(bf16[512,1536]{1,0:T(8,128)(2,1)S(1)} %product.17), channel_id=1, source_target_pairs={{0,1},{3,2},{4,5},{7,6},{8,9},{11,10},{12,13},{15,14},{16,17},{19,... | collective-permute-start | bytes 4718600 | tf_op jit(solution)/shard_map/ppermute | solution.py:212
  187.4 18.8 %collective-permute-done.20 = bf16[512,1536]{1,0:T(8,128)(2,1)} collective-permute-done((bf16[512,1536]{1,0:T(8,128)(2,1)}, bf16[512,1536]{1,0:T(8,128)(2,1)}, u32[]{:S(2)}, u32[]{:S(2)}) %collective-permute-start.20) | collective-permute-done | bytes 1572896 | tf_op jit(solution)/shard_map/ppermute | solution.py:212
  210.5 5.4 %select_bitcast_fusion = (bf16[1,1536,768]{2,1,0:T(8,128)(2,1)}, bf16[1,1536,768]{2,1,0:T(8,128)(2,1)}) fusion(bf16[1536,768]{1,0:T(8,128)(2,1)} %collective-permute-done.4.refs_0_, bf16[1536,768]{1,0:T(8,128)(2,1)} %collective-permute-done.6.refs_1_, pred[]{:T(512)S(6)} %eq.32, bf16[1536,768]{1,0:T(8,128)(2,1)S(1)} %copy-done.22, ...), kind=kLoop, calls=%fused_computation.6 | loop fusion | flops 3538944 | bytes 16515074 | tf_op jit(solution)/shard_map/stack | solution.py:281
  221.9 5.2 %collective-permute-start.17 = (bf16[512,768]{1,0:T(8,128)(2,1)}, bf16[512,768]{1,0:T(8,128)(2,1)S(1)}, u32[]{:S(2)}, u32[]{:S(2)}) collective-permute-start(bf16[512,768]{1,0:T(8,128)(2,1)} %product.18), channel_id=1, source_target_pairs={{0,1},{1,0},{2,3},{3,2},{4,5},{5,4},{6,7},{7,6},{8,9},{9,8},{10,11... | collective-permute-start | bytes 2359304 | tf_op jit(solution)/shard_map/ppermute | solution.py:212
  232.8 23.7 %collective-permute-start.22 = (bf16[512,768]{1,0:T(8,128)(2,1)S(1)}, bf16[512,768]{1,0:T(8,128)(2,1)S(1)}, u32[]{:S(2)}, u32[]{:S(2)}) collective-permute-start(bf16[512,768]{1,0:T(8,128)(2,1)S(1)} %product.20), channel_id=1, source_target_pairs={{0,1},{1,0},{2,3},{3,2},{4,5},{5,4},{6,7},{7,6},{8,9},{9,8},{10,11... | collective-permute-start | bytes 2359304 | tf_op jit(solution)/shard_map/ppermute | solution.py:212
  259.6 14.1 %collective-permute-done.19.refs_6_ = bf16[512,768]{1,0:T(8,128)(2,1)S(1)} collective-permute-done((bf16[512,768]{1,0:T(8,128)(2,1)}, bf16[512,768]{1,0:T(8,128)(2,1)S(1)}, u32[]{:S(2)}, u32[]{:S(2)}) %collective-permute-start.19) | collective-permute-done | bytes 786464 | tf_op jit(solution)/shard_map/ppermute | solution.py:212
  274.6 14.2 %collective-permute-done.22.refs_9_ = bf16[512,768]{1,0:T(8,128)(2,1)S(1)} collective-permute-done((bf16[512,768]{1,0:T(8,128)(2,1)S(1)}, bf16[512,768]{1,0:T(8,128)(2,1)S(1)}, u32[]{:S(2)}, u32[]{:S(2)}) %collective-permute-start.22) | collective-permute-done | bytes 786464 | tf_op jit(solution)/shard_map/ppermute | solution.py:212
  289.9 7.6 %product.21.refs_0_ = bf16[1536,768]{1,0:T(8,128)(2,1)} custom-call(s32[1]{0:T(128)} %bitcast.1.slots, bf16[2,1536,768]{2,1,0:T(8,128)(2,1)} %copy-done, bf16[512,1536]{1,0:T(8,128)(2,1)S(1)} %copy-done.3, bf16[512,1536]{1,0:T(8,128)(2,1)S(1)} %constant_dynamic-update-slice_fusion.2.refs_2_, bf16[512,768]{1,0:T(8,128)(2,1)S(1)} %collective-permute-done.17.refs_3_, ...), custom_call_target="tpu_custom_call" | custom-call | flops 3623878656 | bytes 11796480 | tf_op jit(solution)/shard_map/product/pallas_call | solution.py:151
  303.0 8.1 %collective-permute-done.25.refs_3_ = bf16[512,384]{1,0:T(8,128)(2,1)S(1)} collective-permute-done((bf16[512,384]{1,0:T(8,128)(2,1)S(1)}, bf16[512,384]{1,0:T(8,128)(2,1)S(1)}, u32[]{:S(2)}, u32[]{:S(2)}) %collective-permute-start.25) | collective-permute-done | bytes 393248 | tf_op jit(solution)/shard_map/ppermute | solution.py:212
  312.9 6.4 %collective-permute-done.31.refs_3_ = bf16[512,384]{1,0:T(8,128)(2,1)S(1)} collective-permute-done((bf16[512,384]{1,0:T(8,128)(2,1)}, bf16[512,384]{1,0:T(8,128)(2,1)S(1)}, u32[]{:S(2)}, u32[]{:S(2)}) %collective-permute-start.31) | collective-permute-done | bytes 393248 | tf_op jit(solution)/shard_map/ppermute | solution.py:212
  335.6 4.1 %collective-permute-done.28 = bf16[512,384]{1,0:T(8,128)(2,1)} collective-permute-done((bf16[512,384]{1,0:T(8,128)(2,1)S(1)}, bf16[512,384]{1,0:T(8,128)(2,1)}, u32[]{:S(2)}, u32[]{:S(2)}) %collective-permute-start.28) | collective-permute-done | bytes 393248 | tf_op jit(solution)/shard_map/ppermute | solution.py:209
  341.4 7.3 %collective-permute-done.29 = bf16[512,384]{1,0:T(8,128)(2,1)} collective-permute-done((bf16[512,384]{1,0:T(8,128)(2,1)S(1)}, bf16[512,384]{1,0:T(8,128)(2,1)}, u32[]{:S(2)}, u32[]{:S(2)}) %collective-permute-start.29) | collective-permute-done | bytes 393248 | tf_op jit(solution)/shard_map/ppermute | solution.py:209
  350.1 6.5 %collective-permute-done.33 = bf16[512,384]{1,0:T(8,128)(2,1)S(1)} collective-permute-done((bf16[512,384]{1,0:T(8,128)(2,1)S(1)}, bf16[512,384]{1,0:T(8,128)(2,1)S(1)}, u32[]{:S(2)}, u32[]{:S(2)}) %collective-permute-start.33) | collective-permute-done | bytes 393248 | tf_op jit(solution)/shard_map/ppermute | solution.py:209
  356.6 8.1 %collective-permute-done.34 = bf16[512,384]{1,0:T(8,128)(2,1)S(1)} collective-permute-done((bf16[512,384]{1,0:T(8,128)(2,1)S(1)}, bf16[512,384]{1,0:T(8,128)(2,1)S(1)}, u32[]{:S(2)}, u32[]{:S(2)}) %collective-permute-start.34) | collective-permute-done | bytes 393248 | tf_op jit(solution)/shard_map/ppermute | solution.py:209
  (156 shorter events, 88.2 us)
Async XLA Ops:
  1.9 15.8 %collective-permute-start = (bf16[512,512]{1,0:T(8,128)(2,1)S(1)}, bf16[512,512]{1,0:T(8,128)(2,1)S(1)}, u32[]{:S(2)}, u32[]{:S(2)}) collective-permute-start(bf16[512,512]{1,0:T(8,128)(2,1)S(1)} %constant_dynamic-update-slice_fusion), channel_id=1, source_target_pairs={{0,8},{4,12},{8,0},{12,4},{16,24},{20,28},{24,16},{28,20},{1,9},{5... | collective-permute-start | bytes 1572872 | tf_op jit(solution)/shard_map/ppermute | solution.py:209
  4.9 24.6 %collective-permute-start.1 = (bf16[512,512]{1,0:T(8,128)(2,1)S(1)}, bf16[512,512]{1,0:T(8,128)(2,1)S(1)}, u32[]{:S(2)}, u32[]{:S(2)}) collective-permute-start(bf16[512,512]{1,0:T(8,128)(2,1)S(1)} %constant_dynamic-update-slice_fusion), channel_id=1, source_target_pairs={{0,16},{4,20},{8,24},{12,28},{16,0},{20,4},{24,8},{28,12},{1,17},{... | collective-permute-start | bytes 1572872 | tf_op jit(solution)/shard_map/ppermute | solution.py:209
  6.5 23.9 %collective-permute-start.2 = (bf16[512,512]{1,0:T(8,128)(2,1)S(1)}, bf16[512,512]{1,0:T(8,128)(2,1)}, u32[]{:S(2)}, u32[]{:S(2)}) collective-permute-start(bf16[512,512]{1,0:T(8,128)(2,1)S(1)} %constant_dynamic-update-slice_fusion), channel_id=1, source_target_pairs={{0,24},{4,28},{8,16},{12,20},{16,8},{20,12},{24,0},{28,4},{1,25},{... | collective-permute-start | bytes 1572872 | tf_op jit(solution)/shard_map/ppermute | solution.py:209
  33.1 35.0 %collective-permute-start.3 = (bf16[1536,768]{1,0:T(8,128)(2,1)}, bf16[1536,768]{1,0:T(8,128)(2,1)}, u32[]{:S(2)}, u32[]{:S(2)}) collective-permute-start(bf16[1536,768]{1,0:T(8,128)(2,1)} %get-tuple-element.35.refs_0_), channel_id=1, source_target_pairs={{4,16},{12,24},{16,4},{24,12},{5,17},{13,25},{17,5},{25,13},{6,18}... | collective-permute-start | bytes 7077896 | tf_op jit(solution)/shard_map/ppermute | solution.py:230
  35.3 53.6 %collective-permute-start.4 = (bf16[1536,768]{1,0:T(8,128)(2,1)}, bf16[1536,768]{1,0:T(8,128)(2,1)}, u32[]{:S(2)}, u32[]{:S(2)}) collective-permute-start(bf16[1536,768]{1,0:T(8,128)(2,1)} %get-tuple-element.32), channel_id=1, source_target_pairs={{0,8},{4,24},{8,0},{12,16},{16,12},{20,28},{24,4},{28,20},{1,9},{5... | collective-permute-start | bytes 7077896 | tf_op jit(solution)/shard_map/ppermute | solution.py:230
  37.2 54.8 %collective-permute-start.7 = (bf16[1536,768]{1,0:T(8,128)(2,1)}, bf16[1536,768]{1,0:T(8,128)(2,1)}, u32[]{:S(2)}, u32[]{:S(2)}) collective-permute-start(bf16[1536,768]{1,0:T(8,128)(2,1)} %get-tuple-element.35.refs_0_), channel_id=1, source_target_pairs={{0,4},{8,12},{20,16},{28,24},{1,5},{9,13},{21,17},{29,25},{2,6},{1... | collective-permute-start | bytes 7077896 | tf_op jit(solution)/shard_map/ppermute | solution.py:233
  68.1 25.0 %collective-permute-start.8 = (bf16[1536,768]{1,0:T(8,128)(2,1)}, bf16[1536,768]{1,0:T(8,128)(2,1)}, u32[]{:S(2)}, u32[]{:S(2)}) collective-permute-start(bf16[1536,768]{1,0:T(8,128)(2,1)} %collective-permute-done.3.refs_1_), channel_id=1, source_target_pairs={{4,0},{12,8},{16,20},{24,28},{5,1},{13,9},{17,21},{25,29},{6,2},{1... | collective-permute-start | bytes 7077896 | tf_op jit(solution)/shard_map/ppermute | solution.py:238
  88.9 12.3 %collective-permute-start.6 = (bf16[1536,768]{1,0:T(8,128)(2,1)}, bf16[1536,768]{1,0:T(8,128)(2,1)}, u32[]{:S(2)}, u32[]{:S(2)}) collective-permute-start(bf16[1536,768]{1,0:T(8,128)(2,1)} %collective-permute-done.4.refs_0_), channel_id=1, source_target_pairs={{0,4},{4,0},{8,12},{12,8},{16,20},{20,16},{24,28},{28,24},{1,5},{5... | collective-permute-start | bytes 7077896 | tf_op jit(solution)/shard_map/ppermute | solution.py:209
  90.2 36.4 %collective-permute-start.10 = (bf16[512,1536]{1,0:T(8,128)(2,1)S(1)}, bf16[512,1536]{1,0:T(8,128)(2,1)S(1)}, u32[]{:S(2)}, u32[]{:S(2)}) collective-permute-start(bf16[512,1536]{1,0:T(8,128)(2,1)S(1)} %attend.1.refs_4_.refs_2_.refs_1_), channel_id=1, source_target_pairs={{0,16},{4,20},{8,24},{12,28},{16,0},{20,4},{24,8},{28,12},{1,17},{... | collective-permute-start | bytes 4718600 | tf_op jit(solution)/shard_map/ppermute | solution.py:209
  91.5 36.5 %collective-permute-start.9 = (bf16[512,1536]{1,0:T(8,128)(2,1)S(1)}, bf16[512,1536]{1,0:T(8,128)(2,1)S(1)}, u32[]{:S(2)}, u32[]{:S(2)}) collective-permute-start(bf16[512,1536]{1,0:T(8,128)(2,1)S(1)} %attend.1.refs_4_.refs_2_.refs_1_), channel_id=1, source_target_pairs={{0,8},{4,12},{8,0},{12,4},{16,24},{20,28},{24,16},{28,20},{1,9},{5... | collective-permute-start | bytes 4718600 | tf_op jit(solution)/shard_map/ppermute | solution.py:209
  97.6 21.4 %collective-permute-start.12 = (bf16[512,768]{1,0:T(8,128)(2,1)S(1)}, bf16[512,768]{1,0:T(8,128)(2,1)S(1)}, u32[]{:S(2)}, u32[]{:S(2)}) collective-permute-start(bf16[512,768]{1,0:T(8,128)(2,1)S(1)} %product.13), channel_id=1, source_target_pairs={{0,1},{3,2},{4,5},{7,6},{8,9},{11,10},{12,13},{15,14},{16,17},{19,... | collective-permute-start | bytes 2359304 | tf_op jit(solution)/shard_map/ppermute | solution.py:212
  105.0 33.8 %collective-permute-start.13 = (bf16[512,768]{1,0:T(8,128)(2,1)S(1)}, bf16[512,768]{1,0:T(8,128)(2,1)S(1)}, u32[]{:S(2)}, u32[]{:S(2)}) collective-permute-start(bf16[512,768]{1,0:T(8,128)(2,1)S(1)} %product.14), channel_id=1, source_target_pairs={{0,1},{3,2},{4,5},{7,6},{8,9},{11,10},{12,13},{15,14},{16,17},{19,... | collective-permute-start | bytes 2359304 | tf_op jit(solution)/shard_map/ppermute | solution.py:212
  119.2 22.2 %collective-permute-start.14 = (bf16[512,768]{1,0:T(8,128)(2,1)S(1)}, bf16[512,768]{1,0:T(8,128)(2,1)S(1)}, u32[]{:S(2)}, u32[]{:S(2)}) collective-permute-start(bf16[512,768]{1,0:T(8,128)(2,1)S(1)} %add_convert_fusion.4), channel_id=1, source_target_pairs={{1,2},{2,1},{5,6},{6,5},{9,10},{10,9},{13,14},{14,13},{17,18},{18,... | collective-permute-start | bytes 2359304 | tf_op jit(solution)/shard_map/ppermute | solution.py:212
  133.9 38.6 %collective-permute-start.15 = (bf16[512,1536]{1,0:T(8,128)(2,1)}, bf16[512,1536]{1,0:T(8,128)(2,1)}, u32[]{:S(2)}, u32[]{:S(2)}) collective-permute-start(bf16[512,1536]{1,0:T(8,128)(2,1)} %product.15), channel_id=1, source_target_pairs={{0,1},{3,2},{4,5},{7,6},{8,9},{11,10},{12,13},{15,14},{16,17},{19,... | collective-permute-start | bytes 4718600 | tf_op jit(solution)/shard_map/ppermute | solution.py:212
  138.5 37.4 %collective-permute-start.11 = (bf16[512,1536]{1,0:T(8,128)(2,1)S(1)}, bf16[512,1536]{1,0:T(8,128)(2,1)S(1)}, u32[]{:S(2)}, u32[]{:S(2)}) collective-permute-start(bf16[512,1536]{1,0:T(8,128)(2,1)S(1)} %attend.1.refs_4_.refs_2_.refs_1_), channel_id=1, source_target_pairs={{0,24},{4,28},{8,16},{12,20},{16,8},{20,12},{24,0},{28,4},{1,25},{... | collective-permute-start | bytes 4718600 | tf_op jit(solution)/shard_map/ppermute | solution.py:209
  139.9 12.6 %collective-permute-start.16 = (bf16[512,768]{1,0:T(8,128)(2,1)}, bf16[512,768]{1,0:T(8,128)(2,1)}, u32[]{:S(2)}, u32[]{:S(2)}) collective-permute-start(bf16[512,768]{1,0:T(8,128)(2,1)} %add_convert_fusion.3), channel_id=1, source_target_pairs={{1,2},{2,1},{5,6},{6,5},{9,10},{10,9},{13,14},{14,13},{17,18},{18,... | collective-permute-start | bytes 2359304 | tf_op jit(solution)/shard_map/ppermute | solution.py:212
  147.4 58.9 %collective-permute-start.20 = (bf16[512,1536]{1,0:T(8,128)(2,1)}, bf16[512,1536]{1,0:T(8,128)(2,1)}, u32[]{:S(2)}, u32[]{:S(2)}) collective-permute-start(bf16[512,1536]{1,0:T(8,128)(2,1)} %product.16), channel_id=1, source_target_pairs={{0,1},{3,2},{4,5},{7,6},{8,9},{11,10},{12,13},{15,14},{16,17},{19,... | collective-permute-start | bytes 4718600 | tf_op jit(solution)/shard_map/ppermute | solution.py:212
  181.1 75.3 %collective-permute-start.23 = (bf16[512,1536]{1,0:T(8,128)(2,1)S(1)}, bf16[512,1536]{1,0:T(8,128)(2,1)}, u32[]{:S(2)}, u32[]{:S(2)}) collective-permute-start(bf16[512,1536]{1,0:T(8,128)(2,1)S(1)} %product.17), channel_id=1, source_target_pairs={{0,1},{3,2},{4,5},{7,6},{8,9},{11,10},{12,13},{15,14},{16,17},{19,... | collective-permute-start | bytes 4718600 | tf_op jit(solution)/shard_map/ppermute | solution.py:212
  186.7 40.4 %collective-permute-start.18 = (bf16[512,1536]{1,0:T(8,128)(2,1)}, bf16[512,1536]{1,0:T(8,128)(2,1)S(1)}, u32[]{:S(2)}, u32[]{:S(2)}) collective-permute-start(bf16[512,1536]{1,0:T(8,128)(2,1)} %add_convert_fusion.2), channel_id=1, source_target_pairs={{1,2},{2,1},{5,6},{6,5},{9,10},{10,9},{13,14},{14,13},{17,18},{18,... | collective-permute-start | bytes 4718600 | tf_op jit(solution)/shard_map/ppermute | solution.py:212
  209.8 20.5 %collective-permute-start.21 = (bf16[512,1536]{1,0:T(8,128)(2,1)}, bf16[512,1536]{1,0:T(8,128)(2,1)S(1)}, u32[]{:S(2)}, u32[]{:S(2)}) collective-permute-start(bf16[512,1536]{1,0:T(8,128)(2,1)} %add_convert_fusion.1), channel_id=1, source_target_pairs={{1,2},{2,1},{5,6},{6,5},{9,10},{10,9},{13,14},{14,13},{17,18},{18,... | collective-permute-start | bytes 4718600 | tf_op jit(solution)/shard_map/ppermute | solution.py:212
  221.9 37.6 %collective-permute-start.17 = (bf16[512,768]{1,0:T(8,128)(2,1)}, bf16[512,768]{1,0:T(8,128)(2,1)S(1)}, u32[]{:S(2)}, u32[]{:S(2)}) collective-permute-start(bf16[512,768]{1,0:T(8,128)(2,1)} %product.18), channel_id=1, source_target_pairs={{0,1},{1,0},{2,3},{3,2},{4,5},{5,4},{6,7},{7,6},{8,9},{9,8},{10,11... | collective-permute-start | bytes 2359304 | tf_op jit(solution)/shard_map/ppermute | solution.py:212
  230.2 43.4 %collective-permute-start.19 = (bf16[512,768]{1,0:T(8,128)(2,1)}, bf16[512,768]{1,0:T(8,128)(2,1)S(1)}, u32[]{:S(2)}, u32[]{:S(2)}) collective-permute-start(bf16[512,768]{1,0:T(8,128)(2,1)} %product.19), channel_id=1, source_target_pairs={{0,1},{1,0},{2,3},{3,2},{4,5},{5,4},{6,7},{7,6},{8,9},{9,8},{10,11... | collective-permute-start | bytes 2359304 | tf_op jit(solution)/shard_map/ppermute | solution.py:212
  232.8 56.0 %collective-permute-start.22 = (bf16[512,768]{1,0:T(8,128)(2,1)S(1)}, bf16[512,768]{1,0:T(8,128)(2,1)S(1)}, u32[]{:S(2)}, u32[]{:S(2)}) collective-permute-start(bf16[512,768]{1,0:T(8,128)(2,1)S(1)} %product.20), channel_id=1, source_target_pairs={{0,1},{1,0},{2,3},{3,2},{4,5},{5,4},{6,7},{7,6},{8,9},{9,8},{10,11... | collective-permute-start | bytes 2359304 | tf_op jit(solution)/shard_map/ppermute | solution.py:212
  258.4 39.1 %collective-permute-start.24 = (bf16[512,1536]{1,0:T(8,128)(2,1)S(1)}, bf16[512,1536]{1,0:T(8,128)(2,1)S(1)}, u32[]{:S(2)}, u32[]{:S(2)}) collective-permute-start(bf16[512,1536]{1,0:T(8,128)(2,1)S(1)} %add_convert_fusion), channel_id=1, source_target_pairs={{1,2},{2,1},{5,6},{6,5},{9,10},{10,9},{13,14},{14,13},{17,18},{18,... | collective-permute-start | bytes 4718600 | tf_op jit(solution)/shard_map/ppermute | solution.py:212
  297.5 27.3 %collective-permute-start.26 = (bf16[1536,768]{1,0:T(8,128)(2,1)}, bf16[1536,768]{1,0:T(8,128)(2,1)}, u32[]{:S(2)}, u32[]{:S(2)}) collective-permute-start(bf16[1536,768]{1,0:T(8,128)(2,1)} %product.21.refs_0_), channel_id=1, source_target_pairs={{0,4},{4,0},{8,12},{12,8},{16,20},{20,16},{24,28},{28,24},{1,5},{5... | collective-permute-start | bytes 7077896 | tf_op jit(solution)/shard_map/ppermute | solution.py:209
  298.6 12.5 %collective-permute-start.25 = (bf16[512,384]{1,0:T(8,128)(2,1)S(1)}, bf16[512,384]{1,0:T(8,128)(2,1)S(1)}, u32[]{:S(2)}, u32[]{:S(2)}) collective-permute-start(bf16[512,384]{1,0:T(8,128)(2,1)S(1)} %product.22), channel_id=1, source_target_pairs={{0,1},{1,0},{2,3},{3,2},{4,5},{5,4},{6,7},{7,6},{8,9},{9,8},{10,11... | collective-permute-start | bytes 1179656 | tf_op jit(solution)/shard_map/ppermute | solution.py:212
  303.0 16.4 %collective-permute-start.31 = (bf16[512,384]{1,0:T(8,128)(2,1)}, bf16[512,384]{1,0:T(8,128)(2,1)S(1)}, u32[]{:S(2)}, u32[]{:S(2)}) collective-permute-start(bf16[512,384]{1,0:T(8,128)(2,1)} %product.24), channel_id=1, source_target_pairs={{0,1},{1,0},{2,3},{3,2},{4,5},{5,4},{6,7},{7,6},{8,9},{9,8},{10,11... | collective-permute-start | bytes 1179656 | tf_op jit(solution)/shard_map/ppermute | solution.py:212
  328.3 20.5 %collective-permute-start.29 = (bf16[512,384]{1,0:T(8,128)(2,1)S(1)}, bf16[512,384]{1,0:T(8,128)(2,1)}, u32[]{:S(2)}, u32[]{:S(2)}) collective-permute-start(bf16[512,384]{1,0:T(8,128)(2,1)S(1)} %get-tuple-element.51), channel_id=1, source_target_pairs={{0,16},{4,20},{8,24},{12,28},{16,0},{20,4},{24,8},{28,12},{1,17},{... | collective-permute-start | bytes 1179656 | tf_op jit(solution)/shard_map/ppermute | solution.py:209
  328.9 21.0 %collective-permute-start.30 = (bf16[512,384]{1,0:T(8,128)(2,1)S(1)}, bf16[512,384]{1,0:T(8,128)(2,1)S(1)}, u32[]{:S(2)}, u32[]{:S(2)}) collective-permute-start(bf16[512,384]{1,0:T(8,128)(2,1)S(1)} %get-tuple-element.52), channel_id=1, source_target_pairs={{0,24},{4,28},{8,16},{12,20},{16,8},{20,12},{24,0},{28,4},{1,25},{... | collective-permute-start | bytes 1179656 | tf_op jit(solution)/shard_map/ppermute | solution.py:209
  333.9 22.6 %collective-permute-start.33 = (bf16[512,384]{1,0:T(8,128)(2,1)S(1)}, bf16[512,384]{1,0:T(8,128)(2,1)S(1)}, u32[]{:S(2)}, u32[]{:S(2)}) collective-permute-start(bf16[512,384]{1,0:T(8,128)(2,1)S(1)} %get-tuple-element.54), channel_id=1, source_target_pairs={{0,8},{4,12},{8,0},{12,4},{16,24},{20,28},{24,16},{28,20},{1,9},{5... | collective-permute-start | bytes 1179656 | tf_op jit(solution)/shard_map/ppermute | solution.py:209
  334.5 30.3 %collective-permute-start.34 = (bf16[512,384]{1,0:T(8,128)(2,1)S(1)}, bf16[512,384]{1,0:T(8,128)(2,1)S(1)}, u32[]{:S(2)}, u32[]{:S(2)}) collective-permute-start(bf16[512,384]{1,0:T(8,128)(2,1)S(1)} %get-tuple-element.55), channel_id=1, source_target_pairs={{0,16},{4,20},{8,24},{12,28},{16,0},{20,4},{24,8},{28,12},{1,17},{... | collective-permute-start | bytes 1179656 | tf_op jit(solution)/shard_map/ppermute | solution.py:209
  339.8 25.1 %collective-permute-start.35 = (bf16[512,384]{1,0:T(8,128)(2,1)S(1)}, bf16[512,384]{1,0:T(8,128)(2,1)S(1)}, u32[]{:S(2)}, u32[]{:S(2)}) collective-permute-start(bf16[512,384]{1,0:T(8,128)(2,1)S(1)} %get-tuple-element.56), channel_id=1, source_target_pairs={{0,24},{4,28},{8,16},{12,20},{16,8},{20,12},{24,0},{28,4},{1,25},{... | collective-permute-start | bytes 1179656 | tf_op jit(solution)/shard_map/ppermute | solution.py:209
  (33 other events, 607.8 us)
